TPU v7x, 32 devices: a whole 2x2x4 slice. The times are simulated.
32 devices in a mesh: dp: 16 (over z, y, core), mp: 2 (over x).
Axes of the slice: x: 2, y: 2, z: 4, core: 2. Of those that a mesh axis runs over, the one named last changes fastest.
Arguments:
- enc_in: bfloat16 [64, 512, 512], P(('dp', 'mp')), may hold values from -6 to 6
- enc_segments: int32 [64, 512], P('dp'), may hold values from 0 to 3, never falling along the last dimension, each value on 1 to 256 neighbouring positions
- enc_pad: int32 [64, 512], P('dp'), may hold values 0 or 1
- enc_buckets: int32 [1023], replicated, may hold values from 0 to 31
- dec_in: bfloat16 [64, 64, 512], P(('dp', 'mp')), may hold values from -6 to 6
- dec_segments: int32 [64, 64], P('dp'), may hold values from 0 to 3, never falling along the last dimension, each value on 1 to 32 neighbouring positions
- dec_buckets: int32 [64], replicated, may hold values from 0 to 31
- enc_cot: bfloat16 [64, 512, 512], P(('dp', 'mp')), may hold values from -6 to 6
- dec_cot: bfloat16 [64, 64, 512], P(('dp', 'mp')), may hold values from -6 to 6
- enc_norm1: float32 [512], replicated, may hold values from 0.1 to 1.9
- enc_query: bfloat16 [512, 512], P(None, 'mp'), may hold values from -0.03125 to 0.03125
- enc_kv: bfloat16 [2, 512, 512], P(None, None, 'mp'), may hold values from -0.25 to 0.25
- enc_out_proj: bfloat16 [512, 512], P('mp'), may hold values from -2 to 2
- enc_bias: bfloat16 [32, 8], P(None, 'mp'), may hold values from -4 to 4
- enc_norm2: float32 [512], replicated, may hold values from 0.1 to 1.9
- enc_ff_in: bfloat16 [512, 2048], P(None, 'mp'), may hold values from -0.25 to 0.25
- enc_ff_out: bfloat16 [2048, 512], P('mp'), may hold values from -0.125 to 0.125
- enc_final: float32 [512], replicated, may hold values from 0.1 to 1.9
- dec_norm1: float32 [512], replicated, may hold values from 0.1 to 1.9
- dec_query: bfloat16 [512, 512], P(None, 'mp'), may hold values from -0.03125 to 0.03125
- dec_kv: bfloat16 [2, 512, 512], P(None, None, 'mp'), may hold values from -0.25 to 0.25
- dec_out_proj: bfloat16 [512, 512], P('mp'), may hold values from -0.75 to 0.75
- dec_bias: bfloat16 [32, 8], P(None, 'mp'), may hold values from -4 to 4
- dec_norm2: float32 [512], replicated, may hold values from 0.1 to 1.9
- cross_query: bfloat16 [512, 512], P(None, 'mp'), may hold values from -0.03125 to 0.03125
- cross_kv: bfloat16 [2, 512, 512], P(None, None, 'mp'), may hold values from -0.25 to 0.25
- cross_out: bfloat16 [512, 512], P('mp'), may hold values from -2 to 2
- dec_norm3: float32 [512], replicated, may hold values from 0.1 to 1.9
- dec_ff_in: bfloat16 [512, 2048], P(None, 'mp'), may hold values from -0.25 to 0.25
- dec_ff_out: bfloat16 [2048, 512], P('mp'), may hold values from -0.125 to 0.125
Outputs:
- enc_out: bfloat16 [64, 512, 512], P(('dp', 'mp'))
- dec_out: bfloat16 [64, 64, 512], P(('dp', 'mp'))
- enc_in_grad: float32 [64, 512, 512], P(('dp', 'mp'))
- dec_in_grad: float32 [64, 64, 512], P(('dp', 'mp'))
- enc_norm1_grad: float32 [512], replicated
- enc_query_grad: float32 [512, 512], P(None, 'mp')
- enc_kv_grad: float32 [2, 512, 512], P(None, None, 'mp')
- enc_out_proj_grad: float32 [512, 512], P('mp')
- enc_bias_grad: float32 [32, 8], P(None, 'mp')
- enc_norm2_grad: float32 [512], replicated
- enc_ff_in_grad: float32 [512, 2048], P(None, 'mp')
- enc_ff_out_grad: float32 [2048, 512], P('mp')
- enc_final_grad: float32 [512], replicated
- dec_norm1_grad: float32 [512], replicated
- dec_query_grad: float32 [512, 512], P(None, 'mp')
- dec_kv_grad: float32 [2, 512, 512], P(None, None, 'mp')
- dec_out_proj_grad: float32 [512, 512], P('mp')
- dec_bias_grad: float32 [32, 8], P(None, 'mp')
- dec_norm2_grad: float32 [512], replicated
- cross_query_grad: float32 [512, 512], P(None, 'mp')
- cross_kv_grad: float32 [2, 512, 512], P(None, None, 'mp')
- cross_out_grad: float32 [512, 512], P('mp')
- dec_norm3_grad: float32 [512], replicated
- dec_ff_in_grad: float32 [512, 2048], P(None, 'mp')
- dec_ff_out_grad: float32 [2048, 512], P('mp')
All inputs are finite; a program needn't handle non-finite values. No bound on the sum of `enc_pad` on one device may be relied on, other than what follows from the above.
Results may differ from a plain program's by a relative error of at most 0.03.
Values may be sent and summed in bfloat16 or wider, within the bound.
No kernel may reach another device: no remote copies, remote signals or barrier semaphores. Data moves between devices by JAX's collectives and lax.ppermute only.
A program may use at most 192 MiB of HBM per device.

v0:
```python
import jax
import jax.numpy as jnp
from jax import lax
from jax.sharding import PartitionSpec as P

masked_value = -1e30
norm_eps = 1e-06
highest = lax.Precision.HIGHEST


def rms_scale(values, gain_vec):
    mean_square = jnp.mean(values * values, axis=-1, keepdims=True)
    return values * lax.rsqrt(mean_square + norm_eps) * gain_vec


def norm_back(values, gain_vec, grad_normed):
    return jax.vjp(rms_scale, values, gain_vec)[1](grad_normed)


def split_heads(values, head_count):
    return values.reshape(values.shape[:-1] + (head_count, values.shape[-1] // head_count))


def bucket_onehot(buckets, bucket_count):
    return (buckets[:, None] == jnp.arange(bucket_count, dtype=jnp.int32)[None, :]).astype(
        jnp.float32
    )


def toeplitz_bias(bias_table, onehot, length):
    offsets = jnp.dot(onehot, bias_table, precision=highest).T
    span_width = 2 * length - 1
    rolled = jnp.roll(offsets, -(length - 1), axis=1)
    repeated = jnp.tile(rolled, (1, length))[:, : length * (span_width - 1)]
    return repeated.reshape(offsets.shape[0], length, span_width - 1)[:, :, :length]


def diagonal_totals(score_block, length):
    head_count = score_block.shape[0]
    flipped = score_block[:, ::-1, :]
    padded = jnp.pad(flipped, ((0, 0), (0, 0), (0, length)))
    flattened = padded.reshape(head_count, 2 * length * length)[:, : length * (2 * length - 1)]
    return jnp.sum(flattened.reshape(head_count, length, 2 * length - 1), axis=1)


def masked_scores(queries, key_rows, pos_bias, allowed):
    scores = (
        jnp.einsum("qhd,khd->hqk", queries, key_rows, preferred_element_type=jnp.float32) + pos_bias
    )
    return jnp.where(allowed[None], scores, masked_value)


def attend_block(queries, key_rows, value_rows, pos_bias, allowed):
    scores = masked_scores(queries, key_rows, pos_bias, allowed)
    row_max = jnp.max(scores, axis=-1, keepdims=True)
    exponents = jnp.exp(scores - row_max)
    totals = jnp.sum(exponents, axis=-1, keepdims=True)
    attn_probs = (exponents / totals).astype(jnp.bfloat16)
    mixed_out = jnp.einsum(
        "hqk,khd->qhd", attn_probs, value_rows, preferred_element_type=jnp.float32
    )
    return (mixed_out.astype(jnp.bfloat16), row_max + jnp.log(totals))


def attend_back(queries, key_rows, value_rows, grad_mixed, log_total, pos_bias, allowed):
    scores = masked_scores(queries, key_rows, pos_bias, allowed)
    attn_probs = jnp.exp(scores - log_total)
    grad_probs = jnp.einsum(
        "qhd,khd->hqk", grad_mixed, value_rows, preferred_element_type=jnp.float32
    )
    inner_dot = jnp.sum(attn_probs * grad_probs, axis=-1, keepdims=True)
    grad_scores = attn_probs * (grad_probs - inner_dot)
    grad_low = grad_scores.astype(jnp.bfloat16)
    grad_queries = jnp.einsum(
        "hqk,khd->qhd", grad_low, key_rows, preferred_element_type=jnp.float32
    )
    grad_keys = jnp.einsum("hqk,qhd->khd", grad_low, queries, preferred_element_type=jnp.float32)
    grad_values = jnp.einsum(
        "hqk,qhd->khd",
        attn_probs.astype(jnp.bfloat16),
        grad_mixed,
        preferred_element_type=jnp.float32,
    )
    return (grad_queries, grad_keys, grad_values, grad_scores)


def query_back(full_normed, grad_query):
    return jnp.einsum("rnd,rni->di", full_normed, grad_query, preferred_element_type=jnp.float32)


def pair_back(full_normed, grad_pair):
    return jnp.einsum("rnd,crni->cdi", full_normed, grad_pair, preferred_element_type=jnp.float32)


def query_term(grad_query, weight_query):
    return jnp.einsum("rni,di->rnd", grad_query, weight_query, preferred_element_type=jnp.float32)


def pair_term(grad_pair, weight_pair):
    return jnp.einsum("crni,cdi->rnd", grad_pair, weight_pair, preferred_element_type=jnp.float32)


def on_device(
    enc_in,
    enc_segments,
    enc_pad,
    enc_buckets,
    dec_in,
    dec_segments,
    dec_buckets,
    enc_cot,
    dec_cot,
    enc_norm1,
    enc_query,
    enc_kv,
    enc_out_proj,
    enc_bias,
    enc_norm2,
    enc_ff_in,
    enc_ff_out,
    enc_final,
    dec_norm1,
    dec_query,
    dec_kv,
    dec_out_proj,
    dec_bias,
    dec_norm2,
    cross_query,
    cross_kv,
    cross_out,
    dec_norm3,
    dec_ff_in,
    dec_ff_out,
):
    row_count = enc_in.shape[0]
    enc_length = enc_in.shape[1]
    dec_length = dec_in.shape[1]

    def spread_rows(values):
        return lax.all_gather(values, "mp", axis=0, tiled=True)

    def branch_out(mixed_full, weight):

        def term_rows(first_row, rows_taken):
            return jnp.einsum("rni,id->rnd", mixed_full, weight, preferred_element_type=jnp.float32)

        return lax.psum_scatter(
            term_rows(jnp.int32(0), lax.axis_size("mp") * row_count).astype(jnp.bfloat16),
            "mp",
            scatter_dimension=0,
            tiled=True,
        ).astype(jnp.float32)

    def gather_grads(grad_res):
        return lax.all_gather(grad_res.astype(jnp.bfloat16), "mp", axis=0, tiled=True)

    def scatter_back(term_rows):
        return lax.psum_scatter(
            term_rows(jnp.int32(0), lax.axis_size("mp") * row_count).astype(jnp.bfloat16),
            "mp",
            scatter_dimension=0,
            tiled=True,
        ).astype(jnp.float32)

    def out_back(grad_res, mixed_full, weight):
        grad_full = gather_grads(grad_res)
        grad_weight = jnp.einsum(
            "rni,rnd->id", mixed_full, grad_full, preferred_element_type=jnp.float32
        )
        grad_mixed = jnp.einsum(
            "rnd,id->rni", grad_full, weight, preferred_element_type=jnp.float32
        )
        return (grad_weight, grad_mixed.astype(jnp.bfloat16))

    def ff_back(grad_res, full_normed, pre_act, act_low, weight_in, weight_out):
        grad_full = gather_grads(grad_res)
        grad_out_weight = jnp.einsum(
            "rnf,rnd->fd", act_low, grad_full, preferred_element_type=jnp.float32
        )
        grad_act = jnp.einsum(
            "rnd,fd->rnf", grad_full, weight_out, preferred_element_type=jnp.float32
        )
        grad_pre = jax.vjp(jax.nn.gelu, pre_act)[1](grad_act)[0].astype(jnp.bfloat16)
        grad_in_weight = jnp.einsum(
            "rnd,rnf->df", full_normed, grad_pre, preferred_element_type=jnp.float32
        )

        def term_rows(first_row, rows_taken):
            return jnp.einsum(
                "rnf,df->rnd", grad_pre, weight_in, preferred_element_type=jnp.float32
            )

        return (scatter_back(term_rows), grad_in_weight, grad_out_weight)

    head_count = enc_bias.shape[1]
    bucket_count = enc_bias.shape[0]
    att_rows = enc_segments.shape[0]
    dec_tokens = att_rows * dec_length
    enc_tokens = att_rows * enc_length
    enc_x = enc_in.astype(jnp.float32)
    full_first = spread_rows(rms_scale(enc_x, enc_norm1).astype(jnp.bfloat16))
    queries = jnp.einsum(
        "rld,di->rli", full_first, enc_query, preferred_element_type=jnp.float32
    ).astype(jnp.bfloat16)
    kv_rows = jnp.einsum(
        "rld,cdi->crli", full_first, enc_kv, preferred_element_type=jnp.float32
    ).astype(jnp.bfloat16)
    enc_onehot = bucket_onehot(enc_buckets, bucket_count)
    enc_pos = toeplitz_bias(enc_bias.astype(jnp.float32), enc_onehot, enc_length)
    enc_starts = jnp.concatenate(
        [jnp.ones((att_rows, 1), jnp.bool_), enc_segments[:, 1:] != enc_segments[:, :-1]], axis=1
    )
    enc_visible = (enc_pad == 1) | enc_starts

    def enc_allowed(row_segments, row_visible):
        return (row_segments[:, None] == row_segments[None, :]) & row_visible[None, :]

    def enc_row(packed):
        row_query, row_keys, row_values, row_segments, row_visible = packed
        return attend_block(
            split_heads(row_query, head_count),
            split_heads(row_keys, head_count),
            split_heads(row_values, head_count),
            enc_pos,
            enc_allowed(row_segments, row_visible),
        )

    enc_mixed, enc_logs = lax.map(
        enc_row, (queries, kv_rows[0], kv_rows[1], enc_segments, enc_visible)
    )
    enc_mixed = enc_mixed.reshape(att_rows, enc_length, -1)
    enc_x1 = enc_x + branch_out(enc_mixed, enc_out_proj)
    full_second = spread_rows(rms_scale(enc_x1, enc_norm2).astype(jnp.bfloat16))
    enc_pre = jnp.einsum("rld,df->rlf", full_second, enc_ff_in, preferred_element_type=jnp.float32)
    enc_act = jax.nn.gelu(enc_pre).astype(jnp.bfloat16)
    enc_y = enc_x1 + branch_out(enc_act, enc_ff_out)
    memory_full = spread_rows(rms_scale(enc_y, enc_final).astype(jnp.bfloat16))
    dec_x = dec_in.astype(jnp.float32)
    full_third = spread_rows(rms_scale(dec_x, dec_norm1).astype(jnp.bfloat16))
    dec_queries = jnp.einsum(
        "rmd,di->rmi", full_third, dec_query, preferred_element_type=jnp.float32
    ).astype(jnp.bfloat16)
    dec_kv_rows = jnp.einsum(
        "rmd,cdi->crmi", full_third, dec_kv, preferred_element_type=jnp.float32
    ).astype(jnp.bfloat16)
    dec_columns = jnp.concatenate([dec_buckets[::-1], jnp.full((dec_length - 1,), -1, jnp.int32)])
    dec_onehot = bucket_onehot(dec_columns, bucket_count)
    dec_small = toeplitz_bias(dec_bias.astype(jnp.float32), dec_onehot, dec_length)
    dec_pos = jnp.tile(dec_small, (1, att_rows, att_rows))
    token_index = jnp.arange(dec_tokens, dtype=jnp.int32)
    token_row = token_index // dec_length
    token_segment = dec_segments.reshape(dec_tokens)
    self_allowed = (
        (token_row[:, None] == token_row[None, :])
        & (token_segment[:, None] == token_segment[None, :])
        & (token_index[None, :] <= token_index[:, None])
    )
    key_row = jnp.arange(enc_tokens, dtype=jnp.int32) // enc_length
    cross_allowed = (
        (token_row[:, None] == key_row[None, :])
        & (token_segment[:, None] == enc_segments.reshape(enc_tokens)[None, :])
        & enc_visible.reshape(enc_tokens)[None, :]
    )
    self_queries = split_heads(dec_queries.reshape(dec_tokens, -1), head_count)
    self_keys = split_heads(dec_kv_rows[0].reshape(dec_tokens, -1), head_count)
    self_values = split_heads(dec_kv_rows[1].reshape(dec_tokens, -1), head_count)
    self_mixed, self_logs = attend_block(
        self_queries, self_keys, self_values, dec_pos, self_allowed
    )
    self_full = self_mixed.reshape(att_rows, dec_length, -1)
    dec_x1 = dec_x + branch_out(self_full, dec_out_proj)
    full_fourth = spread_rows(rms_scale(dec_x1, dec_norm2).astype(jnp.bfloat16))
    cross_queries = jnp.einsum(
        "rmd,di->rmi", full_fourth, cross_query, preferred_element_type=jnp.float32
    ).astype(jnp.bfloat16)
    cross_rows = jnp.einsum(
        "rld,cdi->crli", memory_full, cross_kv, preferred_element_type=jnp.float32
    ).astype(jnp.bfloat16)
    cross_query_heads = split_heads(cross_queries.reshape(dec_tokens, -1), head_count)
    cross_key_heads = split_heads(cross_rows[0].reshape(enc_tokens, -1), head_count)
    cross_value_heads = split_heads(cross_rows[1].reshape(enc_tokens, -1), head_count)
    cross_mixed, cross_logs = attend_block(
        cross_query_heads, cross_key_heads, cross_value_heads, 0.0, cross_allowed
    )
    cross_full = cross_mixed.reshape(att_rows, dec_length, -1)
    dec_x2 = dec_x1 + branch_out(cross_full, cross_out)
    full_fifth = spread_rows(rms_scale(dec_x2, dec_norm3).astype(jnp.bfloat16))
    dec_pre = jnp.einsum("rmd,df->rmf", full_fifth, dec_ff_in, preferred_element_type=jnp.float32)
    dec_act = jax.nn.gelu(dec_pre).astype(jnp.bfloat16)
    dec_x3 = dec_x2 + branch_out(dec_act, dec_ff_out)
    enc_out = enc_y.astype(jnp.bfloat16)
    dec_out = dec_x3.astype(jnp.bfloat16)
    grad_third = dec_cot.astype(jnp.float32)
    grad_ff_normed, dec_ff_in_grad, dec_ff_out_grad = ff_back(
        grad_third, full_fifth, dec_pre, dec_act, dec_ff_in, dec_ff_out
    )
    norm_part, dec_norm3_grad = norm_back(dec_x2, dec_norm3, grad_ff_normed)
    grad_second = grad_third + norm_part
    cross_out_grad, grad_cross_mixed = out_back(grad_second, cross_full, cross_out)
    grad_cross_query, grad_cross_key, grad_cross_value, unused = attend_back(
        cross_query_heads,
        cross_key_heads,
        cross_value_heads,
        split_heads(grad_cross_mixed.reshape(dec_tokens, -1), head_count),
        cross_logs,
        0.0,
        cross_allowed,
    )
    grad_cross_query = grad_cross_query.reshape(att_rows, dec_length, -1).astype(jnp.bfloat16)
    grad_cross_pair = (
        jnp.stack([grad_cross_key, grad_cross_value])
        .reshape(2, att_rows, enc_length, -1)
        .astype(jnp.bfloat16)
    )
    cross_query_grad = query_back(full_fourth, grad_cross_query)
    cross_kv_grad = pair_back(memory_full, grad_cross_pair)
    grad_cross_normed = scatter_back(
        lambda first_row, rows_taken: query_term(grad_cross_query, cross_query)
    )
    grad_memory = scatter_back(lambda first_row, rows_taken: pair_term(grad_cross_pair, cross_kv))
    norm_part, dec_norm2_grad = norm_back(dec_x1, dec_norm2, grad_cross_normed)
    grad_first = grad_second + norm_part
    dec_out_proj_grad, grad_self_mixed = out_back(grad_first, self_full, dec_out_proj)
    grad_self_query, grad_self_key, grad_self_value, grad_self_scores = attend_back(
        self_queries,
        self_keys,
        self_values,
        split_heads(grad_self_mixed.reshape(dec_tokens, -1), head_count),
        self_logs,
        dec_pos,
        self_allowed,
    )
    folded = jnp.sum(
        grad_self_scores.reshape(head_count, att_rows, dec_length, att_rows, dec_length),
        axis=(1, 3),
    )
    dec_bias_grad = jnp.einsum(
        "cb,hc->bh", dec_onehot, diagonal_totals(folded, dec_length), precision=highest
    )
    grad_self_query = grad_self_query.reshape(att_rows, dec_length, -1).astype(jnp.bfloat16)
    grad_self_pair = (
        jnp.stack([grad_self_key, grad_self_value])
        .reshape(2, att_rows, dec_length, -1)
        .astype(jnp.bfloat16)
    )
    dec_query_grad = query_back(full_third, grad_self_query)
    dec_kv_grad = pair_back(full_third, grad_self_pair)
    grad_self_normed = scatter_back(
        lambda first_row, rows_taken: query_term(grad_self_query, dec_query)
        + pair_term(grad_self_pair, dec_kv)
    )
    norm_part, dec_norm1_grad = norm_back(dec_x, dec_norm1, grad_self_normed)
    dec_in_grad = grad_first + norm_part
    norm_part, enc_final_grad = norm_back(enc_y, enc_final, grad_memory)
    grad_output = enc_cot.astype(jnp.float32) + norm_part
    grad_second_normed, enc_ff_in_grad, enc_ff_out_grad = ff_back(
        grad_output, full_second, enc_pre, enc_act, enc_ff_in, enc_ff_out
    )
    norm_part, enc_norm2_grad = norm_back(enc_x1, enc_norm2, grad_second_normed)
    grad_middle = grad_output + norm_part
    enc_out_proj_grad, grad_enc_mixed = out_back(grad_middle, enc_mixed, enc_out_proj)

    def enc_row_back(packed):
        row_query, row_keys, row_values, row_grad, row_logs, row_segments, row_visible = packed
        grad_query, grad_key, grad_value, grad_scores = attend_back(
            split_heads(row_query, head_count),
            split_heads(row_keys, head_count),
            split_heads(row_values, head_count),
            split_heads(row_grad, head_count),
            row_logs,
            enc_pos,
            enc_allowed(row_segments, row_visible),
        )
        return (
            grad_query.astype(jnp.bfloat16),
            grad_key.astype(jnp.bfloat16),
            grad_value.astype(jnp.bfloat16),
            diagonal_totals(grad_scores, enc_length),
        )

    grad_enc_query, grad_enc_key, grad_enc_value, enc_diagonals = lax.map(
        enc_row_back,
        (queries, kv_rows[0], kv_rows[1], grad_enc_mixed, enc_logs, enc_segments, enc_visible),
    )
    enc_bias_grad = jnp.einsum(
        "cb,hc->bh", enc_onehot, jnp.sum(enc_diagonals, axis=0), precision=highest
    )
    grad_enc_query = grad_enc_query.reshape(att_rows, enc_length, -1)
    grad_enc_pair = jnp.stack([grad_enc_key, grad_enc_value]).reshape(2, att_rows, enc_length, -1)
    enc_query_grad = query_back(full_first, grad_enc_query)
    enc_kv_grad = pair_back(full_first, grad_enc_pair)
    grad_first_normed = scatter_back(
        lambda first_row, rows_taken: query_term(grad_enc_query, enc_query)
        + pair_term(grad_enc_pair, enc_kv)
    )
    norm_part, enc_norm1_grad = norm_back(enc_x, enc_norm1, grad_first_normed)
    enc_in_grad = grad_middle + norm_part
    (
        enc_norm1_grad,
        enc_norm2_grad,
        enc_final_grad,
        dec_norm1_grad,
        dec_norm2_grad,
        dec_norm3_grad,
    ) = lax.psum(
        (
            enc_norm1_grad,
            enc_norm2_grad,
            enc_final_grad,
            dec_norm1_grad,
            dec_norm2_grad,
            dec_norm3_grad,
        ),
        ("dp", "mp"),
    )
    (
        enc_query_grad,
        enc_kv_grad,
        enc_out_proj_grad,
        enc_bias_grad,
        enc_ff_in_grad,
        enc_ff_out_grad,
        dec_query_grad,
        dec_kv_grad,
        dec_out_proj_grad,
        dec_bias_grad,
        cross_query_grad,
        cross_kv_grad,
        cross_out_grad,
        dec_ff_in_grad,
        dec_ff_out_grad,
    ) = lax.psum(
        (
            enc_query_grad,
            enc_kv_grad,
            enc_out_proj_grad,
            enc_bias_grad,
            enc_ff_in_grad,
            enc_ff_out_grad,
            dec_query_grad,
            dec_kv_grad,
            dec_out_proj_grad,
            dec_bias_grad,
            cross_query_grad,
            cross_kv_grad,
            cross_out_grad,
            dec_ff_in_grad,
            dec_ff_out_grad,
        ),
        "dp",
    )
    return (
        enc_out,
        dec_out,
        enc_in_grad,
        dec_in_grad,
        enc_norm1_grad,
        enc_query_grad,
        enc_kv_grad,
        enc_out_proj_grad,
        enc_bias_grad,
        enc_norm2_grad,
        enc_ff_in_grad,
        enc_ff_out_grad,
        enc_final_grad,
        dec_norm1_grad,
        dec_query_grad,
        dec_kv_grad,
        dec_out_proj_grad,
        dec_bias_grad,
        dec_norm2_grad,
        cross_query_grad,
        cross_kv_grad,
        cross_out_grad,
        dec_norm3_grad,
        dec_ff_in_grad,
        dec_ff_out_grad,
    )


def solution(mesh):
    in_specs = (
        P(("dp", "mp"), None, None),
        P("dp", None),
        P("dp", None),
        P(),
        P(("dp", "mp"), None, None),
        P("dp", None),
        P(),
        P(("dp", "mp"), None, None),
        P(("dp", "mp"), None, None),
        P(),
        P(None, "mp"),
        P(None, None, "mp"),
        P("mp", None),
        P(None, "mp"),
        P(),
        P(None, "mp"),
        P("mp", None),
        P(),
        P(),
        P(None, "mp"),
        P(None, None, "mp"),
        P("mp", None),
        P(None, "mp"),
        P(),
        P(None, "mp"),
        P(None, None, "mp"),
        P("mp", None),
        P(),
        P(None, "mp"),
        P("mp", None),
    )
    out_specs = (
        P(("dp", "mp"), None, None),
        P(("dp", "mp"), None, None),
        P(("dp", "mp"), None, None),
        P(("dp", "mp"), None, None),
        P(),
        P(None, "mp"),
        P(None, None, "mp"),
        P("mp", None),
        P(None, "mp"),
        P(),
        P(None, "mp"),
        P("mp", None),
        P(),
        P(),
        P(None, "mp"),
        P(None, None, "mp"),
        P("mp", None),
        P(None, "mp"),
        P(),
        P(None, "mp"),
        P(None, None, "mp"),
        P("mp", None),
        P(),
        P(None, "mp"),
        P("mp", None),
    )
    return jax.shard_map(
        on_device, mesh=mesh, in_specs=in_specs, out_specs=out_specs, check_vma=False
    )
```

profile of v0, /device:TPU:0, one launch (start us, length us, event | category | flops | bytes accessed | tf_op | source)
XLA Modules:
  0.0 1318.5 jit_solution(6930446565583013603)
XLA Ops:
  17.4 15.0 %tile.13 = f32[4,523776]{1,0:T(4,128)} reshape(f32[4,512,1023]{2,1,0:T(8,128)} %tile.12) | data formatting | bytes 16760832 | tf_op jit(solution)/shard_map/tile | solution.py:34
  40.0 15.8 %reshape.629 = f32[4,512,1022]{2,1,0:T(8,128)} reshape(f32[4,523264]{1,0:T(4,128)} %slice.85) | data formatting | bytes 16744448 | tf_op jit(solution)/shard_map/reshape | solution.py:35
  76.7 28.8 %while.30 = (s32[]{:T(128)}, bf16[4,512,4,64]{1,3,2,0:T(8,128)(2,1)}, f32[4,4,512,1]{2,1,3,0:T(4,128)}, bf16[4,512,256]{1,2,0:T(8,128)(2,1)S(1)}, s32[4,512]{1,0...) while((s32[]{:T(128)}, ...), condition=%wide.region_4.5_spmd, body=%wide.region_1.4_spmd.sunk | while | flops 277477376 | bytes 19996292 | solution.py:228
  110.0 34.9 %reduce-scatter.12.cloned.1.call-done = bf16[2,512,512]{2,1,0:T(8,128)(2,1)} async-done(((bf16[4,512,512]{2,1,0:T(8,128)(2,1)}), bf16[2,512,512]{2,1,0:T(8,128)(2,1)}) %reduce-scatter.12.cloned.1.call-update) | async-done | bytes 1048592 | tf_op jit(solution)/shard_map/reduce_scatter | solution.py:147
  148.1 33.2 %all-gather.8.cloned.1.call-done = bf16[4,512,512]{2,1,0:T(8,128)(2,1)} async-done(((bf16[2,512,512]{2,1,0:T(8,128)(2,1)}), bf16[4,512,512]{2,1,0:T(8,128)(2,1)}) %all-gather.8.cloned.1.call-update) | async-done | bytes 2097168 | tf_op jit(solution)/shard_map/all_gather | solution.py:140
  262.5 21.7 %all-gather.10.cloned.1.call-done = bf16[4,512,512]{2,1,0:T(8,128)(2,1)} async-done(((bf16[2,512,512]{2,1,0:T(8,128)(2,1)}), bf16[4,512,512]{2,1,0:T(8,128)(2,1)}) %all-gather.10.cloned.1.call-update) | async-done | bytes 2097168 | tf_op jit(solution)/shard_map/all_gather | solution.py:140
  407.8 31.8 %reduce-scatter.24.cloned.1.call-done = bf16[2,512,512]{2,1,0:T(8,128)(2,1)} async-done(((bf16[4,512,512]{2,1,0:T(8,128)(2,1)}), bf16[2,512,512]{2,1,0:T(8,128)(2,1)}) %reduce-scatter.24.cloned.1.call-update) | async-done | bytes 1048592 | tf_op jit(solution)/shard_map/reduce_scatter | solution.py:158
  456.5 23.0 %all-gather.12.cloned.1.call-done = bf16[4,512,512]{2,1,0:T(8,128)(2,1)} async-done(((bf16[2,512,512]{2,1,0:T(8,128)(2,1)}), bf16[4,512,512]{2,1,0:T(8,128)(2,1)}) %all-gather.12.cloned.1.call-update) | async-done | bytes 2097168 | tf_op jit(solution)/shard_map/all_gather | solution.py:155
  499.7 28.9 %reduce-scatter.26.cloned.1.call-done = bf16[2,512,512]{2,1,0:T(8,128)(2,1)} async-done(((bf16[4,512,512]{2,1,0:T(8,128)(2,1)}), bf16[2,512,512]{2,1,0:T(8,128)(2,1)}) %reduce-scatter.26.cloned.1.call-update) | async-done | bytes 1048592 | tf_op jit(solution)/shard_map/reduce_scatter | solution.py:158
  552.7 16.3 %all-gather.14.cloned.1.call-done = bf16[4,512,512]{2,1,0:T(8,128)(2,1)} async-done(((bf16[2,512,512]{2,1,0:T(8,128)(2,1)}), bf16[4,512,512]{2,1,0:T(8,128)(2,1)}) %all-gather.14.cloned.1.call-update) | async-done | bytes 2097168 | tf_op jit(solution)/shard_map/all_gather | solution.py:155
  573.6 389.3 %while.31 = (s32[]{:T(128)}, bf16[4,512,4,64]{1,3,2,0:T(8,128)(2,1)}, bf16[4,512,4,64]{1,3,2,0:T(8,128)(2,1)}, bf16[4,512,4,64]{1,3,2,0:T(8,128)(2,1)S(1)}, f32[...) while((s32[]{:T(128)}, ...), condition=%wide.region_29.30_spmd, body=%wide.region_26.29_spmd.sunk | while | flops 684580864 | bytes 169402064 | solution.py:381
  585.7 34.3 %rev.15 = f32[4,512,512]{1,2,0:T(8,128)} reverse(f32[4,512,512]{1,2,0:T(8,128)} %copy-done.2), dimensions={1} | reverse | bytes 8388608 | tf_op jit(solution)/shard_map/while/body/eval_jaxpr/rev | solution.py:40
  650.9 15.8 %reshape.679 = f32[4,512,1023]{2,1,0:T(8,128)} reshape(f32[4,523776]{1,0:T(4,128)} %slice.103) | data formatting | bytes 16760832 | tf_op jit(solution)/shard_map/while/body/eval_jaxpr/reshape | solution.py:43
  682.9 34.3 %rev.15 = f32[4,512,512]{1,2,0:T(8,128)} reverse(f32[4,512,512]{1,2,0:T(8,128)} %copy-done.2), dimensions={1} | reverse | bytes 8388608 | tf_op jit(solution)/shard_map/while/body/eval_jaxpr/rev | solution.py:40
  748.1 15.8 %reshape.679 = f32[4,512,1023]{2,1,0:T(8,128)} reshape(f32[4,523776]{1,0:T(4,128)} %slice.103) | data formatting | bytes 16760832 | tf_op jit(solution)/shard_map/while/body/eval_jaxpr/reshape | solution.py:43
  780.1 34.3 %rev.15 = f32[4,512,512]{1,2,0:T(8,128)} reverse(f32[4,512,512]{1,2,0:T(8,128)} %copy-done.2), dimensions={1} | reverse | bytes 8388608 | tf_op jit(solution)/shard_map/while/body/eval_jaxpr/rev | solution.py:40
  826.2 12.1 copy.326
  845.3 15.8 %reshape.679 = f32[4,512,1023]{2,1,0:T(8,128)} reshape(f32[4,523776]{1,0:T(4,128)} %slice.103) | data formatting | bytes 16760832 | tf_op jit(solution)/shard_map/while/body/eval_jaxpr/reshape | solution.py:43
  877.3 34.3 %rev.15 = f32[4,512,512]{1,2,0:T(8,128)} reverse(f32[4,512,512]{1,2,0:T(8,128)} %copy-done.2), dimensions={1} | reverse | bytes 8388608 | tf_op jit(solution)/shard_map/while/body/eval_jaxpr/rev | solution.py:40
  923.4 12.1 copy.326
  942.5 15.8 %reshape.679 = f32[4,512,1023]{2,1,0:T(8,128)} reshape(f32[4,523776]{1,0:T(4,128)} %slice.103) | data formatting | bytes 16760832 | tf_op jit(solution)/shard_map/while/body/eval_jaxpr/reshape | solution.py:43
  1021.8 35.9 %all-reduce.5 = (f32[32,4]{0,1:T(4,128)}, f32[32,4]{0,1:T(4,128)}) all-reduce(f32[32,4]{0,1:T(4,128)S(1)} %fusion.120, f32[32,4]{0,1:T(4,128)} %fusion.159), channel_id=1, replica_groups=mesh['dp'=16,'mp'=2] {'dp'}, use_global_device_ids=true, to_apply=%region_43.44 | all-reduce | flops 256 | bytes 2048 | tf_op jit(solution)/shard_map/psum | solution.py:432
  1060.0 38.8 %all-reduce.4 = (f32[512]{0:T(512)}, f32[512]{0:T(512)}, f32[512]{0:T(512)}, f32[512]{0:T(512)}, f32[512]{0:T(512)}, /*index=5*/f32[512]{0:T(512)}) all-reduce(f32[512]{0:T(512)S(1)} %get-tuple-element.435, f32[512]{0:T(512)S(1)} %copy-done.142, f32[512]{0:T(512)S(1)} %copy-done.139, ...), channel_id=1, replica_groups=mesh['dp'=16,'mp'=2] {'dp','mp'}, use_global_device_ids=true, to_apply=%region_38.39 | all-reduce | flops 3072 | bytes 24576 | tf_op jit(solution)/shard_map/psum | solution.py:405
  1103.8 188.3 %all-reduce.9.cloned.1.call-done = (f32[512,256]{1,0:T(8,128)}, f32[2,512,256]{1,2,0:T(8,128)}, f32[256,512]{1,0:T(8,128)}, f32[512,1024]{1,0:T(8,128)}, f32[102...) async-done(((f32[512,256]{1,0:T(8,128)}, ...) | async-done | bytes 14680080 | tf_op jit(solution)/shard_map/psum | solution.py:432
  (679 shorter events, 593.7 us)
Async XLA Ops:
  7.2 181.7 %copy-start = (bf16[1024,512]{1,0:T(8,128)(2,1)S(1)}, bf16[1024,512]{1,0:T(8,128)(2,1)}, u32[]{:S(2)}) copy-start(bf16[1024,512]{1,0:T(8,128)(2,1)} %param.50) | copy-start | bytes 3145732
  7.2 58.7 %all-gather.6.cloned.1.call-start = ((), (), s32[]{:S(2)}) async-start(), calls=%async_computation.11 | async-start | bytes 3145728 | tf_op jit(solution)/shard_map/all_gather | solution.py:140
  12.6 132.3 %reduce-scatter.12.cloned.1.call-start = ((), (), s32[]{:S(2)}) async-start(), calls=%async_computation.12 | async-start | bytes 3145728 | tf_op jit(solution)/shard_map/reduce_scatter | solution.py:147
  109.9 71.4 %all-gather.8.cloned.1.call-start = ((), (), s32[]{:S(2)}) async-start(), calls=%async_computation.13 | async-start | bytes 3145728 | tf_op jit(solution)/shard_map/all_gather | solution.py:140
  148.1 89.1 %reduce-scatter.14.cloned.1.call-start = ((), (), s32[]{:S(2)}) async-start(), calls=%async_computation.14 | async-start | bytes 3145728 | tf_op jit(solution)/shard_map/reduce_scatter | solution.py:147
  192.9 56.0 %reduce-scatter.16.cloned.1.call-start = ((), (), s32[]{:S(2)}) async-start(), calls=%async_computation.15 | async-start | bytes 393216 | tf_op jit(solution)/shard_map/reduce_scatter | solution.py:147
  237.1 47.0 %all-gather.10.cloned.1.call-start = ((), (), s32[]{:S(2)}) async-start(), calls=%async_computation.16 | async-start | bytes 3145728 | tf_op jit(solution)/shard_map/all_gather | solution.py:140
  239.1 292.6 %copy-start.100 = (f32[2,512]{1,0:T(2,128)}, f32[2,512]{1,0:T(2,128)S(1)}, u32[]{:S(2)}) copy-start(f32[2,512]{1,0:T(2,128)S(1)} %fusion.168) | copy-start | bytes 12292
  240.6 85.8 %reduce-scatter.18.cloned.1.call-start = ((), (), s32[]{:S(2)}) async-start(), calls=%async_computation.17 | async-start | bytes 393216 | tf_op jit(solution)/shard_map/reduce_scatter | solution.py:147
  314.6 37.6 %reduce-scatter.22.cloned.1.call-start = ((), (), s32[]{:S(2)}) async-start(), calls=%async_computation.19 | async-start | bytes 393216 | tf_op jit(solution)/shard_map/reduce_scatter | solution.py:158
  340.5 99.1 %reduce-scatter.24.cloned.1.call-start = ((), (), s32[]{:S(2)}) async-start(), calls=%async_computation.20 | async-start | bytes 3145728 | tf_op jit(solution)/shard_map/reduce_scatter | solution.py:158
  407.6 72.0 %all-gather.12.cloned.1.call-start = ((), (), s32[]{:S(2)}) async-start(), calls=%async_computation.21 | async-start | bytes 3145728 | tf_op jit(solution)/shard_map/all_gather | solution.py:155
  446.3 50.6 %reduce-scatter.30.cloned.1.call-start = ((), (), s32[]{:S(2)}) async-start(), calls=%async_computation.25 | async-start | bytes 393216 | tf_op jit(solution)/shard_map/reduce_scatter | solution.py:158
  456.5 72.2 %reduce-scatter.26.cloned.1.call-start = ((), (), s32[]{:S(2)}) async-start(), calls=%async_computation.22 | async-start | bytes 3145728 | tf_op jit(solution)/shard_map/reduce_scatter | solution.py:158
  495.5 73.6 %all-gather.14.cloned.1.call-start = ((), (), s32[]{:S(2)}) async-start(), calls=%async_computation.23 | async-start | bytes 3145728 | tf_op jit(solution)/shard_map/all_gather | solution.py:155
  535.8 478.7 %reduce-scatter.32.cloned.1.call-start = ((), (), s32[]{:S(2)}) async-start(), calls=%async_computation.26 | async-start | bytes 393216 | tf_op jit(solution)/shard_map/reduce_scatter | solution.py:158
  550.2 467.1 %reduce-scatter.20.cloned.1.call-start = ((), (), s32[]{:S(2)}) async-start(), calls=%async_computation.18 | async-start | bytes 393216 | tf_op jit(solution)/shard_map/reduce_scatter | solution.py:147
  552.7 505.0 %reduce-scatter.28.cloned.1.call-start = ((), (), s32[]{:S(2)}) async-start(), calls=%async_computation.24 | async-start | bytes 3145728 | tf_op jit(solution)/shard_map/reduce_scatter | solution.py:158
  573.6 389.4 %copy-start.87 = (bf16[512,256]{1,0:T(8,128)(2,1)S(1)}, bf16[512,256]{1,0:T(8,128)(2,1)}, u32[]{:S(2)}) copy-start(bf16[512,256]{1,0:T(8,128)(2,1)} %param.44) | copy-start | bytes 786436
  974.5 317.6 %all-reduce.9.cloned.1.call-start = ((), (), s32[]{:S(2)}) async-start(), calls=%async_computation.27 | async-start | bytes 29360128 | tf_op jit(solution)/shard_map/psum | solution.py:432
  1012.8 86.0 %copy-start.13 = (bf16[2,512,512]{2,1,0:T(8,128)(2,1)S(1)}, bf16[2,512,512]{2,1,0:T(8,128)(2,1)}, u32[]{:S(2)}) copy-start(bf16[2,512,512]{2,1,0:T(8,128)(2,1)} %reduce-scatter.14.cloned.1.call-done) | copy-start | bytes 3145732
  1012.8 86.0 %copy-start.101 = (f32[2,512]{1,0:T(2,128)S(1)}, f32[2,512]{1,0:T(2,128)}, u32[]{:S(2)}) copy-start(f32[2,512]{1,0:T(2,128)} %copy-done.100) | copy-start | bytes 12292
  1012.8 86.0 %copy-start.104 = (f32[2,512]{1,0:T(2,128)S(1)}, f32[2,512]{1,0:T(2,128)}, u32[]{:S(2)}) copy-start(f32[2,512]{1,0:T(2,128)} %copy-done.102) | copy-start | bytes 12292
  1012.8 86.0 %copy-start.110 = (f32[2,512]{1,0:T(2,128)S(1)}, f32[2,512]{1,0:T(2,128)}, u32[]{:S(2)}) copy-start(f32[2,512]{1,0:T(2,128)} %copy-done.108) | copy-start | bytes 12292
  (155 other events, 1511.1 us)
Sparse Core Ops, SparseCore 0:
  12.7 35.8 all-gather.5
  110.1 34.8 reduce-scatter.11
  148.2 33.1 all-gather.7
  193.0 34.6 reduce-scatter.13
  237.2 11.6 reduce-scatter.15
  251.0 33.1 all-gather.9
  314.8 11.6 reduce-scatter.17
  340.6 11.6 reduce-scatter.21
  407.7 31.8 reduce-scatter.23
  446.4 33.1 all-gather.11
  482.3 11.6 reduce-scatter.29
  496.8 31.8 reduce-scatter.25
  535.9 33.1 all-gather.13
  571.7 11.6 reduce-scatter.31
  585.5 11.7 reduce-scatter.19
  974.6 31.8 reduce-scatter.27
  1015.7 276.3 all-reduce.8
where the time goes:
time: 1340 us; the launch traced here: 1320 us
  local copies, waits for them, and re-layouts  517 us (39%)
  waiting for transfers between devices  401 us (30%)
  matrix products  177 us (13%)
  blocking collectives  114 us (9%)
  other arithmetic  91.6 us (7%)
  between operations  15.7 us (1%)
    psum x1, waiting for transfers between devices, on_device(): lax.psum((enc_query_grad, enc_kv_grad, enc_out_proj_grad, enc_bias_grad,...  188 us
    rev x5, local copies, waits for them, and re-layouts, diagonal_totals(): flipped = score_block[:, ::-1, :]  138 us
    while x28, local copies, waits for them, and re-layouts  101 us
    reduce_scatter x6, waiting for transfers between devices, scatter_back(): lax.psum_scatter(term_rows(jnp.int32(0), lax.axis_size('mp') * row_count)...  71.2 us
    reshape x5, local copies, waits for them, and re-layouts, diagonal_totals(): flattened.reshape(head_count, length, 2 * length - 1)  63.3 us
    all_gather x3, waiting for transfers between devices, spread_rows(): return lax.all_gather(values, 'mp', axis=0, tiled=True)  54.9 us
    reduce_scatter x5, waiting for transfers between devices, branch_out(): lax.psum_scatter(term_rows(jnp.int32(0), lax.axis_size('mp') * row_count)...  46.8 us
    unnamed x326, local copies, waits for them, and re-layouts  44.4 us
  transfers between devices with their start and end apart: 17, of which 11 were waited for; matrix products, arithmetic and copies ran while one was open for 44% of the time, Pallas kernels for 0%

commit v1 on v0

v1 whole, which is shorter than its diff:
```python
import functools

import jax
import jax.numpy as jnp
from jax import lax
from jax.experimental import pallas as pl
from jax.experimental.pallas import tpu as pltpu
from jax.sharding import PartitionSpec as P

f32 = jnp.float32
bf16 = jnp.bfloat16
neg = -1e30
eps = 1e-06
LANE = 128
MIB = 1 << 20


def nn(a, b):
    return lax.dot_general(a, b, (((1,), (0,)), ((), ())), preferred_element_type=f32)


def nt(a, b):
    return lax.dot_general(a, b, (((1,), (1,)), ((), ())), preferred_element_type=f32)


def tn(a, b):
    return lax.dot_general(a, b, (((0,), (0,)), ((), ())), preferred_element_type=f32)


def total(terms):
    return functools.reduce(lambda a, b: a + b, terms)


def rms_parts(v):
    r = lax.rsqrt(jnp.mean(v * v, axis=-1, keepdims=True) + eps)
    return v * r, r


def rms(v, g):
    return (rms_parts(v)[0] * g).astype(bf16)


def rms_back(v, g, dn):
    vr, r = rms_parts(v)
    dg = jnp.sum(dn * vr, axis=0, keepdims=True)
    t = dn * g
    return r * (t - vr * jnp.mean(t * vr, axis=-1, keepdims=True)), dg


def gelu_both(u):
    c = 0.7978845608028654
    u2 = u * u
    t = jnp.tanh(u * (c + (c * 0.044715) * u2))
    half = 0.5 + 0.5 * t
    slope = half + (0.5 * u) * (1.0 - t * t) * (c + (3 * c * 0.044715) * u2)
    return u * half, slope


def params(vmem_mib=56, **kw):
    return pltpu.CompilerParams(vmem_limit_bytes=vmem_mib * MIB, **kw)


def cost(flops, nbytes):
    return pl.CostEstimate(flops=int(flops), bytes_accessed=int(nbytes), transcendentals=0)


def whole(a):
    return pl.BlockSpec(a.shape, lambda *_: (0,) * a.ndim, pipeline_mode=pl.Buffered(1))


def sds(shape, dtype):
    return jax.ShapeDtypeStruct(shape, dtype)


class Flat:
    def __init__(self, layout):
        self.at, row = {}, 0
        for name, kind in layout:
            self.at[name] = (row, kind)
            row += {"out": 256, "up": 1024, "down": 1024, "pair": 512, "one": 256, "tabs": 32}[kind]
        self.rows = row
        self.layout = layout

    def pack(self, arrays):
        parts = []
        for name, kind in self.layout:
            a = arrays[name]
            if kind in ("out", "down"):
                parts.append(a)
            elif kind == "up":
                parts += [a[:, :512], a[:, 512:]]
            elif kind == "pair":
                parts.append(jnp.concatenate([a[0], a[1]], axis=1))
            elif kind == "tabs":
                parts.append(
                    jnp.concatenate(
                        [jnp.pad(t, ((0, 0), (0, 256 - t.shape[1]))) for t in a], axis=1
                    )
                )
            else:
                parts.append(jnp.concatenate([a[:256], a[256:]], axis=1))
        return jnp.concatenate(parts, axis=0)


enc_qkv = Flat([("qk", "pair"), ("v", "one")])
enc_qkv_tabs = Flat([("qk", "pair"), ("v", "one"), ("tabs", "tabs")])
enc_mid = Flat([("ffo", "down"), ("ffi", "up"), ("ckv", "pair"), ("out", "out")])
dec_all = Flat(
    [
        ("ffo", "down"),
        ("ffi", "up"),
        ("cout", "out"),
        ("cq", "one"),
        ("out", "out"),
        ("qk", "pair"),
        ("v", "one"),
    ]
)


def bring(ids_ref, pieces, full, sems):
    n = len(pieces)
    size = full.shape[0] // n
    own = ids_ref[2] if n == 2 else ids_ref[3]
    copies = []
    for p, piece in enumerate(pieces):
        at = pl.multiple_of((p ^ own) * size, 16)
        copies.append(pltpu.make_async_copy(piece, full.at[pl.ds(at, size), :], sems.at[p]))
    for c in copies:
        c.start()
    for c in copies:
        c.wait()


def one_mul(a, w):
    return nn(a[:, :256], w[:, :256]) + nn(a[:, 256:], w[:, 256:])


def one_back(g, w):
    return jnp.concatenate([nt(g, w[:, :256]), nt(g, w[:, 256:])], axis=1)


def one_grad(a, g):
    full = tn(a, g)
    return jnp.concatenate([full[:256], full[256:]], axis=1)


def bucket_rows(rev_ref):
    rev = pltpu.roll(rev_ref[...], 1024 - 127, 1)
    return lax.broadcasted_iota(jnp.int32, (32, 1024), 0) == rev


def skew_rows(tab, rev_ref, skew_ref):
    w = tn(tab, bucket_rows(rev_ref).astype(bf16))
    for h in range(w.shape[0]):
        base = jnp.broadcast_to(w[h : h + 1], (LANE, 1024))
        skew_ref[h] = pltpu.roll(base, 0, 1, stride=1, stride_axis=0)


def diagonal_sums(a):
    rows, n = a.shape
    while rows > 1:
        rows //= 2
        a = a[:rows] + pltpu.roll(a[rows:], n - rows, 1)
    return a


def key_codes(seg, pad):
    start = (lax.broadcasted_iota(jnp.int32, seg.shape, 1) == 0) | (seg != pltpu.roll(seg, 1, 1))
    segf = seg.astype(f32)
    return segf, jnp.where((pad == 1) | start, segf, -1.0)


def as_column(row):
    return jnp.transpose(jnp.broadcast_to(row, (LANE, row.shape[1])))


def mask_add(seg, pad, out_ref):
    code, key = key_codes(seg, pad)
    keyc = as_column(key)
    for b in range(seg.shape[1] // LANE):
        out_ref[:, b * LANE : (b + 1) * LANE] = jnp.where(
            keyc == code[:, b * LANE : (b + 1) * LANE], 0.0, neg
        )


def pad_half(a_t, low):
    z = jnp.zeros_like(a_t)
    return jnp.concatenate([a_t, z] if low else [z, a_t], axis=0)


def skew_block(skew_ref, h, q0, width, keys=512):
    return jnp.concatenate(
        [
            skew_ref[h, :, 384 - LANE * b + q0 : 384 - LANE * b + q0 + width]
            for b in range(keys // LANE)
        ],
        axis=0,
    )


QB = 256


def enc_fwd_kernel(own, ids_ref, x_ref, g_ref, seg_ref, pad_ref, rev_ref, *rest):
    step = pl.program_id(0)
    if own:
        tab_ref, wq_ref, wkv_ref, qkv_ref, o_ref, lse_ref, skew, madd, o_t = rest
    else:
        p0, p1, qkv_ref, o_ref, lse_ref, w_ref, tab_ref, skew, madd, o_t, sems = rest

        @pl.when(step == 0)
        def _():
            bring(ids_ref, (p0, p1), w_ref, sems)
            tab_ref[...] = w_ref[768:800, :]

    @pl.when(step == 0)
    def _():
        skew_rows(tab_ref[:, 0:4], rev_ref, skew)

    row = pl.ds(ids_ref[1] + step, 1)
    mask_add(seg_ref[row, :], pad_ref[row, :], madd)
    n1 = rms(x_ref[0].astype(f32), g_ref[...])
    if own:
        q = nn(n1, wq_ref[...]).astype(bf16)
        k = nn(n1, wkv_ref[0]).astype(bf16)
        v = nn(n1, wkv_ref[1]).astype(bf16)
    else:
        qk = nn(n1, w_ref[0:512, :]).astype(bf16)
        q, k = qk[:, :256], qk[:, 256:]
        v = one_mul(n1, w_ref[512:768, :]).astype(bf16)
    qkv_ref[0, :, 0:256] = q
    qkv_ref[0, :, 256:512] = k
    qkv_ref[0, :, 512:768] = v
    q_t, v_t = jnp.transpose(q), jnp.transpose(v)
    for h in range(4):
        pair = slice(LANE * (h // 2), LANE * (h // 2) + LANE)
        rows = slice(64 * h, 64 * h + 64)
        k2 = k[:, pair]
        qz = pad_half(q_t[rows], h % 2 == 0)
        for b in range(0, 512, QB):
            s = nn(k2, qz[:, b : b + QB]) + skew_block(skew, h, b, QB) + madd[:, b : b + QB]
            m = jnp.max(s, axis=0, keepdims=True)
            e = jnp.exp(s - m)
            norm = jnp.sum(e, axis=0, keepdims=True)
            o_t[rows, b : b + QB] = nn(v_t[rows], e.astype(bf16)) * (1.0 / norm)
            lse_ref[0, h : h + 1, b : b + QB] = m + jnp.log(norm)
    o_ref[0] = jnp.transpose(o_t[...]).astype(bf16)


smem = pl.BlockSpec(memory_space=pltpu.SMEM)
anywhere = pl.BlockSpec(memory_space=pl.ANY)


def row_block(width, n=512, at=0):
    return pl.BlockSpec((1, n, width), lambda r: (r, 0, at))


def enc_fwd(ids, x, g, seg, pad, rev, ws):
    rows = x.shape[0]
    own = len(ws) == 3
    more = [] if own else [sds((enc_qkv_tabs.rows, 512), bf16), sds((32, 512), bf16)]
    return pl.pallas_call(
        functools.partial(enc_fwd_kernel, own),
        name="enc_attend_own" if own else "enc_attend_other",
        grid=(rows,),
        in_specs=[smem, row_block(512), whole(g), whole(seg), whole(pad), whole(rev)]
        + [whole(w) if own else anywhere for w in ws],
        out_specs=[row_block(768), row_block(256), row_block(512, 4)] + [whole(a) for a in more],
        out_shape=[
            sds((rows, 512, 768), bf16),
            sds((rows, 512, 256), bf16),
            sds((rows, 4, 512), f32),
        ]
        + more,
        scratch_shapes=[
            pltpu.VMEM((4, LANE, 1024), f32),
            pltpu.VMEM((512, 512), f32),
            pltpu.VMEM((256, 512), f32),
        ]
        + ([] if own else [pltpu.SemaphoreType.DMA((2,))]),
        compiler_params=params(),
        cost_estimate=cost(8e9, 4e6),
    )(ids, x, g, seg, pad, rev, *ws)


def enc_bwd_kernel(
    rows_n,
    ids_ref,
    x_ref,
    g_ref,
    seg_ref,
    pad_ref,
    rev_ref,
    tab_ref,
    qkv_ref,
    o_ref,
    do_ref,
    lse_ref,
    dqkv_ref,
    keep_ref,
    send_ref,
    dtab_ref,
    skew,
    dskew,
    madd,
    p_s,
    ds_s,
    dq_t,
    dv_acc,
    dk_acc,
    acc,
):
    step = pl.program_id(0)

    @pl.when(step == 0)
    def _():
        skew_rows(tab_ref[:, 0:4], rev_ref, skew)
        dskew[...] = jnp.zeros_like(dskew)

    row = pl.ds(ids_ref[1] + step, 1)
    mask_add(seg_ref[row, :], pad_ref[row, :], madd)
    q, k, v = qkv_ref[0, :, 0:256], qkv_ref[0, :, 256:512], qkv_ref[0, :, 512:768]
    do = do_ref[0]
    q_t, k_t, do_t = jnp.transpose(q), jnp.transpose(k), jnp.transpose(do)
    o_t = jnp.transpose(o_ref[0])
    lane = lax.broadcasted_iota(jnp.int32, (512, LANE), 1)
    for h in range(4):
        pair = slice(LANE * (h // 2), LANE * (h // 2) + LANE)
        rows = slice(64 * h, 64 * h + 64)
        low = h % 2 == 0
        k2, v2 = k[:, pair], v[:, pair]
        qz, doz = pad_half(q_t[rows], low), pad_half(do_t[rows], low)
        inner = jnp.sum(
            do_t[rows].astype(f32) * o_t[rows].astype(f32), axis=0, keepdims=True
        )
        for b in range(0, 512, QB):
            cols = slice(b, b + QB)
            s = nn(k2, qz[:, cols]) + skew_block(skew, h, b, QB) + madd[:, cols]
            p = jnp.exp(s - lse_ref[0, h : h + 1, cols])
            ds = p * (nn(v2, doz[:, cols]) - inner[:, cols])
            p_s[:, cols] = p.astype(bf16)
            ds_s[:, cols] = ds.astype(bf16)
            for kb in range(4):
                at = 384 - LANE * kb + b
                dskew[h, :, at : at + QB] += ds[LANE * kb : LANE * kb + LANE]
        mine = (lane < 64) if low else (lane >= 64)
        dv2 = nn(p_s[...], jnp.where(mine, do[:, pair], jnp.zeros((), bf16)))
        dk2 = nn(ds_s[...], jnp.where(mine, q[:, pair], jnp.zeros((), bf16)))
        if low:
            dv_acc[:, pair] = dv2
            dk_acc[:, pair] = dk2
        else:
            dv_acc[:, pair] += dv2
            dk_acc[:, pair] += dk2
        dq_t[rows] = nn(k_t[rows], ds_s[...])
    dqkv_ref[0, :, 0:256] = jnp.transpose(dq_t[...]).astype(bf16)
    dqkv_ref[0, :, 256:512] = dk_acc[...].astype(bf16)
    dqkv_ref[0, :, 512:768] = dv_acc[...].astype(bf16)
    n1_t = jnp.transpose(rms(x_ref[0].astype(f32), g_ref[...]))
    dqk = nn(n1_t, dqkv_ref[0, :, 0:512])
    dv = nn(n1_t, dqkv_ref[0, :, 512:768])
    dv = jnp.concatenate([dv[:256], dv[256:]], axis=1)

    @pl.when(step == 0)
    def _():
        acc[0:512] = dqk
        acc[512:768] = dv

    @pl.when(step > 0)
    def _():
        acc[0:512] += dqk
        acc[512:768] += dv

    @pl.when(step == rows_n - 1)
    def _():
        place(ids_ref, acc, keep_ref, send_ref)
        onehot = bucket_rows(rev_ref)
        out_lane = lax.broadcasted_iota(jnp.int32, (32, LANE), 1)
        dtab = jnp.zeros((32, LANE), f32)
        for h in range(4):
            diag = diagonal_sums(dskew[h])
            col = jnp.sum(jnp.where(onehot, diag, 0.0), axis=1, keepdims=True)
            dtab = dtab + jnp.where(out_lane == h, col, 0.0)
        dtab_ref[...] = dtab


def place(ids_ref, acc, keep_ref, send_ref):
    chunks = 16
    size = acc.shape[0] // chunks
    own = ids_ref[0]
    high = own // 8
    low = own % 8
    for j in range(chunks):
        at = pl.multiple_of(((j % 8) ^ low) * size, 16)
        piece = acc[j * size : (j + 1) * size].astype(bf16)

        @pl.when(high == j // 8)
        def _():
            keep_ref[pl.ds(at, size), :] = piece

        @pl.when(high != j // 8)
        def _():
            send_ref[pl.ds(at, size), :] = piece


def enc_bwd(half_at, ids, x, g, seg, pad, rev, tab, qkv, o, do, lse):
    rows = x.shape[0]
    half = enc_qkv.rows // 2
    return pl.pallas_call(
        functools.partial(enc_bwd_kernel, rows),
        name="enc_attend_other_back" if half_at else "enc_attend_own_back",
        grid=(rows,),
        in_specs=[
            smem,
            row_block(512),
            whole(g),
            whole(seg),
            whole(pad),
            whole(rev),
            whole(tab),
            row_block(768),
            row_block(256),
            row_block(256, at=half_at),
            row_block(512, 4),
        ],
        out_specs=[
            row_block(768),
            pl.BlockSpec((half, 512), lambda r: (0, 0)),
            pl.BlockSpec((half, 512), lambda r: (0, 0)),
            pl.BlockSpec((32, LANE), lambda r: (0, 0)),
        ],
        out_shape=[
            sds((rows, 512, 768), bf16),
            sds((half, 512), bf16),
            sds((half, 512), bf16),
            sds((32, LANE), f32),
        ],
        scratch_shapes=[
            pltpu.VMEM((4, LANE, 1024), f32),
            pltpu.VMEM((4, LANE, 1024), f32),
            pltpu.VMEM((512, 512), f32),
            pltpu.VMEM((512, 512), bf16),
            pltpu.VMEM((512, 512), bf16),
            pltpu.VMEM((256, 512), f32),
            pltpu.VMEM((512, 256), f32),
            pltpu.VMEM((512, 256), f32),
            pltpu.VMEM((enc_qkv.rows, 512), f32),
        ],
        compiler_params=params(),
        cost_estimate=cost(16e9, 8e6),
    )(ids, x, g, seg, pad, rev, tab, qkv, o, do, lse)


class Mid:
    def __init__(self, refs):
        if len(refs) == 1:
            (w,) = refs
            at = {n: r for n, (r, _) in enc_mid.at.items()}
            self.ffo = lambda c: w[at["ffo"] + 512 * c : at["ffo"] + 512 * c + 512, :]
            self.ffi = lambda c: w[at["ffi"] + 512 * c : at["ffi"] + 512 * c + 512, :]
            self.ckv = lambda c: w[at["ckv"] : at["ckv"] + 512, 256 * c : 256 * c + 256]
            self.out = lambda: w[at["out"] : at["out"] + 256, :]
        else:
            ffo, ffi, ckv, out = refs
            self.ffo = lambda c: ffo[512 * c : 512 * c + 512, :]
            self.ffi = lambda c: ffi[:, 512 * c : 512 * c + 512]
            self.ckv = lambda c: ckv[c]
            self.out = lambda: out[...]


def mid_fwd_kernel(ids_ref, x_ref, oa_ref, ob_ref, g2_ref, gf_ref, *rest):
    pieces = rest[4:8]
    x1_ref, y_ref, out_ref, h_ref, gp_ref, kv_ref, w_ref, sems = rest[8:]
    halves = (Mid(rest[:4]), Mid([w_ref]))

    @pl.when(pl.program_id(0) == 0)
    def _():
        bring(ids_ref, pieces, w_ref, sems)

    x1 = x_ref[...].astype(f32) + total(
        [nn(oa_ref[...], halves[0].out()), nn(ob_ref[...], halves[1].out())]
    )
    x1_ref[...] = x1
    m1 = rms(x1, g2_ref[...])
    terms = []
    for i, w in enumerate(halves):
        for c in range(2):
            u = nn(m1, w.ffi(c))
            h, slope = gelu_both(u)
            h = h.astype(bf16)
            cols = slice(1024 * i + 512 * c, 1024 * i + 512 * c + 512)
            h_ref[:, cols] = h
            gp_ref[:, cols] = slope.astype(bf16)
            terms.append(nn(h, w.ffo(c)))
    y = x1 + total(terms)
    y_ref[...] = y
    out_ref[...] = y.astype(bf16)
    mem = rms(y, gf_ref[...])
    for c in range(2):
        for i, w in enumerate(halves):
            at = 512 * c + 256 * i
            kv_ref[:, at : at + 256] = nn(mem, w.ckv(c)).astype(bf16)


def tile_block(tile, width):
    return pl.BlockSpec((tile, width), lambda t: (t, 0))


def mid_fwd(ids, x, oa, ob, g2, gf, own, pieces, tile=256):
    n = x.shape[0]
    return pl.pallas_call(
        mid_fwd_kernel,
        name="enc_middle",
        grid=(n // tile,),
        in_specs=[smem, tile_block(tile, 512), tile_block(tile, 256), tile_block(tile, 256), whole(g2), whole(gf)]
        + [whole(w) for w in own]
        + [anywhere] * len(pieces),
        out_specs=[
            tile_block(tile, 512),
            tile_block(tile, 512),
            tile_block(tile, 512),
            tile_block(tile, 2048),
            tile_block(tile, 2048),
            tile_block(tile, 1024),
            whole(sds((enc_mid.rows, 512), bf16)),
        ],
        out_shape=[
            sds((n, 512), f32),
            sds((n, 512), f32),
            sds((n, 512), bf16),
            sds((n, 2048), bf16),
            sds((n, 2048), bf16),
            sds((n, 1024), bf16),
            sds((enc_mid.rows, 512), bf16),
        ],
        scratch_shapes=[pltpu.SemaphoreType.DMA((len(pieces),))],
        compiler_params=params(),
        cost_estimate=cost(10e9, 2e7),
    )(ids, x, oa, ob, g2, gf, *own, *pieces)


def mid_bwd_kernel(steps, dkv_ref, y_ref, cot_ref, x1_ref, h_ref, gp_ref, oa_ref, ob_ref, g2_ref, gf_ref, ids_ref, *rest):
    halves = (Mid(rest[:4]), Mid(rest[4:5]))
    dx1_ref, do_ref, ka_ref, sa_ref, kb_ref, sb_ref, dg2_ref, dgf_ref, acc_a, acc_b = rest[5:]
    accs = (acc_a, acc_b)
    step = pl.program_id(0)
    at = {n: r for n, (r, _) in enc_mid.at.items()}

    def add(i, row, value, lanes=slice(None)):
        rows = slice(row, row + value.shape[0])

        @pl.when(step == 0)
        def _():
            accs[i][rows, lanes] = value

        @pl.when(step > 0)
        def _():
            accs[i][rows, lanes] += value

    y = y_ref[...]
    mem = rms(y, gf_ref[...])
    terms = []
    for i, w in enumerate(halves):
        for c in range(2):
            d = dkv_ref[:, 512 * c + 256 * i : 512 * c + 256 * i + 256]
            terms.append(nt(d, w.ckv(c)))
            add(i, at["ckv"], tn(mem, d), slice(256 * c, 256 * c + 256))
    part, dgf = rms_back(y, gf_ref[...], total(terms))
    dy = cot_ref[...].astype(f32) + part
    g = dy.astype(bf16)
    x1 = x1_ref[...]
    m1 = rms(x1, g2_ref[...])
    terms = []
    for i, w in enumerate(halves):
        for c in range(2):
            cols = slice(1024 * i + 512 * c, 1024 * i + 512 * c + 512)
            du = (nt(g, w.ffo(c)) * gp_ref[:, cols].astype(f32)).astype(bf16)
            add(i, at["ffo"] + 512 * c, tn(h_ref[:, cols], g))
            add(i, at["ffi"] + 512 * c, tn(m1, du))
            terms.append(nt(du, w.ffi(c)))
    part, dg2 = rms_back(x1, g2_ref[...], total(terms))
    dx1 = dy + part
    dx1_ref[...] = dx1
    g = dx1.astype(bf16)
    for i, (w, o_ref) in enumerate(zip(halves, (oa_ref, ob_ref))):
        do_ref[:, 256 * i : 256 * i + 256] = nt(g, w.out()).astype(bf16)
        add(i, at["out"], tn(o_ref[...], g))

    @pl.when(step == 0)
    def _():
        dg2_ref[...] = dg2
        dgf_ref[...] = dgf

    @pl.when(step > 0)
    def _():
        dg2_ref[...] += dg2
        dgf_ref[...] += dgf

    @pl.when(step == steps - 1)
    def _():
        place(ids_ref, acc_a, ka_ref, sa_ref)
        place(ids_ref, acc_b, kb_ref, sb_ref)


def mid_bwd(dkv, y, cot, x1, h, gp, oa, ob, g2, gf, pos, own, oth, tile=512):
    n = y.shape[0]
    ws = list(own) + [oth]
    half = enc_mid.rows // 2
    fixed = lambda shape: pl.BlockSpec(shape, lambda t: (0, 0), pipeline_mode=pl.Buffered(1))
    return pl.pallas_call(
        functools.partial(mid_bwd_kernel, n // tile),
        name="enc_middle_back",
        grid=(n // tile,),
        in_specs=[
            tile_block(tile, 1024),
            tile_block(tile, 512),
            tile_block(tile, 512),
            tile_block(tile, 512),
            tile_block(tile, 2048),
            tile_block(tile, 2048),
            tile_block(tile, 256),
            tile_block(tile, 256),
            whole(g2),
            whole(gf),
            pl.BlockSpec(memory_space=pltpu.SMEM),
        ]
        + [whole(w) for w in ws],
        out_specs=[tile_block(tile, 512), tile_block(tile, 512)]
        + [fixed((half, 512))] * 4
        + [fixed((1, 512))] * 2,
        out_shape=[sds((n, 512), f32), sds((n, 512), bf16)]
        + [sds((half, 512), bf16)] * 4
        + [sds((1, 512), f32)] * 2,
        scratch_shapes=[pltpu.VMEM((enc_mid.rows, 512), f32)] * 2,
        compiler_params=params(60),
        cost_estimate=cost(22e9, 3e7),
    )(dkv, y, cot, x1, h, gp, oa, ob, g2, gf, pos, *ws)


def enc_last_kernel(x_ref, dx1_ref, da_ref, db_ref, g_ref, wq_ref, wkv_ref, w_ref, out_ref, dg_ref):
    step = pl.program_id(0)
    da, db = da_ref[...], db_ref[...]
    dn = (
        nt(da[:, 0:256], wq_ref[...])
        + nt(da[:, 256:512], wkv_ref[0])
        + nt(da[:, 512:768], wkv_ref[1])
        + nt(db[:, 0:512], w_ref[0:512, :])
        + one_back(db[:, 512:768], w_ref[512:768, :])
    )
    part, dg = rms_back(x_ref[...].astype(f32), g_ref[...], dn)
    out_ref[...] = dx1_ref[...] + part

    @pl.when(step == 0)
    def _():
        dg_ref[...] = dg

    @pl.when(step > 0)
    def _():
        dg_ref[...] += dg


def enc_last(x, dx1, da, db, g, own, oth, tile=256):
    n = x.shape[0]
    ws = list(own) + [oth]
    return pl.pallas_call(
        enc_last_kernel,
        name="enc_input_back",
        grid=(n // tile,),
        in_specs=[
            tile_block(tile, 512),
            tile_block(tile, 512),
            tile_block(tile, 768),
            tile_block(tile, 768),
            whole(g),
        ]
        + [whole(w) for w in ws],
        out_specs=[tile_block(tile, 512), pl.BlockSpec((1, 512), lambda t: (0, 0))],
        out_shape=[sds((n, 512), f32), sds((1, 512), f32)],
        compiler_params=params(),
        cost_estimate=cost(4e9, 1e7),
    )(x, dx1, da, db, g, *ws)


class Dec:
    def __init__(self, refs):
        if len(refs) == 1:
            (w,) = refs
            at = {n: r for n, (r, _) in dec_all.at.items()}
            self.ffo = lambda c: w[at["ffo"] + 512 * c : at["ffo"] + 512 * c + 512, :]
            self.ffi = lambda c: w[at["ffi"] + 512 * c : at["ffi"] + 512 * c + 512, :]
            self.cout = lambda: w[at["cout"] : at["cout"] + 256, :]
            self.cq = lambda c: w[at["cq"] : at["cq"] + 256, 256 * c : 256 * c + 256]
            self.out = lambda: w[at["out"] : at["out"] + 256, :]
            self.qk = lambda c: w[at["qk"] : at["qk"] + 512, 256 * c : 256 * c + 256]
            self.v = lambda c: w[at["v"] : at["v"] + 256, 256 * c : 256 * c + 256]
        else:
            ffo, ffi, cout, cq, out, q, kv = refs
            self.ffo = lambda c: ffo[512 * c : 512 * c + 512, :]
            self.ffi = lambda c: ffi[:, 512 * c : 512 * c + 512]
            self.cout = lambda: cout[...]
            self.cq = lambda c: cq[256 * c : 256 * c + 256, :]
            self.out = lambda: out[...]
            self.qk = lambda c: q[...] if c == 0 else kv[0]
            self.v = lambda c: kv[1, 256 * c : 256 * c + 256, :]


def two_mul(a, w):
    return nn(a[:, :256], w(0)) + nn(a[:, 256:], w(1))


def two_back(g, w):
    return jnp.concatenate([nt(g, w(0)), nt(g, w(1))], axis=1)


def spread_t(a_t, width):
    tiled = jnp.concatenate([a_t] * 4, axis=1)
    head = lax.broadcasted_iota(jnp.int32, tiled.shape, 0) // 64
    block = lax.broadcasted_iota(jnp.int32, tiled.shape, 1) // width
    return jnp.where(head == block, tiled, jnp.zeros((), a_t.dtype))


def spread(a, height):
    tiled = jnp.concatenate([a] * 4, axis=0)
    block = lax.broadcasted_iota(jnp.int32, tiled.shape, 0) // height
    head = lax.broadcasted_iota(jnp.int32, tiled.shape, 1) // 64
    return jnp.where(head == block, tiled, jnp.zeros((), a.dtype))


def fold(full, height):
    head = lax.broadcasted_iota(jnp.int32, (height, 256), 1) // 64
    total = jnp.zeros((height, 256), f32)
    for h in range(4):
        total = total + jnp.where(head == h, full[height * h : height * h + height], 0.0)
    return total


def dec_bucket_rows(buckets_ref):
    b = buckets_ref[...]
    b = jnp.concatenate([b, jnp.full((1, LANE - b.shape[1]), -1, jnp.int32)], axis=1)
    return lax.broadcasted_iota(jnp.int32, (32, LANE), 0) == b


def dec_bias_rows(tab, buckets_ref):
    w = tn(tab, dec_bucket_rows(buckets_ref).astype(bf16))
    return jnp.concatenate(
        [
            pltpu.roll(jnp.broadcast_to(w[h : h + 1], (LANE, LANE)), 0, 1, stride=1, stride_axis=0)
            for h in range(4)
        ],
        axis=1,
    )


def dec_self_mask(ids_ref, dseg_ref, rows):
    code = jnp.concatenate(
        [(dseg_ref[pl.ds(ids_ref[1] + r, 1), :] + 8 * r).astype(f32) for r in range(rows)], axis=1
    )
    key = as_column(code)
    j = lax.broadcasted_iota(jnp.int32, (LANE, LANE), 0)
    i = lax.broadcasted_iota(jnp.int32, (LANE, LANE), 1)
    one = jnp.where((key == code) & (j <= i), 0.0, neg)
    return jnp.concatenate([one] * 4, axis=1)


def dec_first_kernel(ids_ref, x_ref, g1_ref, g2_ref, dseg_ref, buckets_ref, taba_ref, tabb_ref, *rest):
    pieces = rest[7:11]
    qkv_ref, o_ref, lse_ref, z1_ref, q3_ref, w_ref, sems = rest[11:]
    halves = (Dec(rest[:7]), Dec([w_ref]))
    bring(ids_ref, pieces, w_ref, sems)
    z = x_ref[...].astype(f32)
    n2 = rms(z, g1_ref[...])
    mask = dec_self_mask(ids_ref, dseg_ref, x_ref.shape[0] // 64)
    terms = []
    for i, (w, tab) in enumerate(zip(halves, (taba_ref[...], tabb_ref[:, 256:260]))):
        q = nn(n2, w.qk(0)).astype(bf16)
        k = nn(n2, w.qk(1)).astype(bf16)
        v = two_mul(n2, w.v).astype(bf16)
        for c, a in enumerate((q, k, v)):
            qkv_ref[:, 512 * c + 256 * i : 512 * c + 256 * i + 256] = a
        s = nn(k, spread_t(jnp.transpose(q), LANE)) + dec_bias_rows(tab, buckets_ref) + mask
        m = jnp.max(s, axis=0, keepdims=True)
        e = jnp.exp(s - m)
        norm = jnp.sum(e, axis=0, keepdims=True)
        p = (e * (1.0 / norm)).astype(bf16)
        lse_ref[i : i + 1, :] = m + jnp.log(norm)
        o = fold(tn(p, v), LANE).astype(bf16)
        o_ref[:, 256 * i : 256 * i + 256] = o
        terms.append(nn(o, w.out()))
    z1 = z + total(terms)
    z1_ref[...] = z1
    n3 = rms(z1, g2_ref[...])
    for i, w in enumerate(halves):
        q3_ref[:, 256 * i : 256 * i + 256] = two_mul(n3, w.cq).astype(bf16)


def dec_first(ids, x, g1, g2, dseg, buckets, taba, tabb, own, pieces):
    n = x.shape[0]
    ins = [x, g1, g2, dseg, buckets, taba, tabb, *own]
    return pl.pallas_call(
        dec_first_kernel,
        name="dec_self",
        grid=(1,),
        in_specs=[smem] + [whole(a) for a in ins] + [anywhere] * len(pieces),
        out_specs=[
            pl.BlockSpec(s, lambda t: (0, 0))
            for s in ((n, 1536), (n, 512), (2, 512), (n, 512), (n, 512), (dec_all.rows, 512))
        ],
        out_shape=[
            sds((n, 1536), bf16),
            sds((n, 512), bf16),
            sds((2, 512), f32),
            sds((n, 512), f32),
            sds((n, 512), bf16),
            sds((dec_all.rows, 512), bf16),
        ],
        scratch_shapes=[pltpu.SemaphoreType.DMA((len(pieces),))],
        compiler_params=params(),
        cost_estimate=cost(1e9, 8e6),
    )(ids, *ins, *pieces)


def dec_main_kernel(
    x_ref,
    cot_ref,
    g1_ref,
    g2_ref,
    g3_ref,
    buckets_ref,
    dseg_ref,
    seg_ref,
    pad_ref,
    ids_ref,
    qkv_ref,
    o2_ref,
    lse_ref,
    z1_ref,
    q3_ref,
    kv_ref,
    taba_ref,
    tabb_ref,
    *rest,
):
    halves = (Dec(rest[:7]), Dec(rest[7:8]))
    out_ref, dx_ref, dkv_ref, ka_ref, sa_ref, kb_ref, sb_ref, dg_ref, dtab_ref = rest[8:17]
    madd, p_s, acc_a, acc_b = rest[17:]
    accs = (acc_a, acc_b)
    at = {n: r for n, (r, _) in dec_all.at.items()}
    rows_n = x_ref.shape[0] // 64
    z1 = z1_ref[...]
    mixed = [[None] * rows_n, [None] * rows_n]
    for r in range(rows_n):
        row = pl.ds(ids_ref[1] + r, 1)
        keyc = as_column(key_codes(seg_ref[row, :], pad_ref[row, :])[1])
        code = dseg_ref[row, :].astype(f32)
        madd[...] = jnp.where(keyc == jnp.concatenate([code, code], axis=1), 0.0, neg)
        both = jnp.concatenate([madd[...]] * 2, axis=1)
        for i in range(2):
            cols = slice(256 * i, 256 * i + 256)
            k3 = kv_ref[512 * r : 512 * r + 512, 256 * i : 256 * i + 256]
            v3 = kv_ref[512 * r : 512 * r + 512, 512 + 256 * i : 512 + 256 * i + 256]
            q_t = jnp.transpose(q3_ref[64 * r : 64 * r + 64, cols])
            s = nn(k3, spread_t(q_t, 64)) + both
            m = jnp.max(s, axis=0, keepdims=True)
            e = jnp.exp(s - m)
            p = e * (1.0 / jnp.sum(e, axis=0, keepdims=True))
            p_s[2 * r + i] = p
            mixed[i][r] = fold(tn(p.astype(bf16), v3), 64).astype(bf16)
    o3 = [jnp.concatenate(m, axis=0) for m in mixed]
    z2 = z1 + total([nn(o, w.cout()) for o, w in zip(o3, halves)])
    n4 = rms(z2, g3_ref[...])
    terms, kept = [], []
    for i, w in enumerate(halves):
        for c in range(2):
            h, slope = gelu_both(nn(n4, w.ffi(c)))
            h = h.astype(bf16)
            kept.append((h, slope))
            terms.append(nn(h, w.ffo(c)))
    out_ref[...] = (z2 + total(terms)).astype(bf16)
    g = cot_ref[...]
    terms = []
    for i, w in enumerate(halves):
        for c in range(2):
            h, slope = kept[2 * i + c]
            accs[i][at["ffo"] + 512 * c : at["ffo"] + 512 * c + 512] = tn(h, g)
            du = (nt(g, w.ffo(c)) * slope).astype(bf16)
            accs[i][at["ffi"] + 512 * c : at["ffi"] + 512 * c + 512] = tn(n4, du)
            terms.append(nt(du, w.ffi(c)))
    part, dg3 = rms_back(z2, g3_ref[...], total(terms))
    dz2 = g.astype(f32) + part
    g = dz2.astype(bf16)
    n3 = rms(z1, g2_ref[...])
    terms = []
    for i, w in enumerate(halves):
        cols = slice(256 * i, 256 * i + 256)
        accs[i][at["cout"] : at["cout"] + 256] = tn(o3[i], g)
        do = nt(g, w.cout()).astype(bf16)
        dq = []
        for r in range(rows_n):
            k3 = kv_ref[512 * r : 512 * r + 512, 256 * i : 256 * i + 256]
            v3 = kv_ref[512 * r : 512 * r + 512, 512 + 256 * i : 512 + 256 * i + 256]
            do_r = do[64 * r : 64 * r + 64]
            p = p_s[2 * r + i]
            dp = nn(v3, spread_t(jnp.transpose(do_r), 64))
            ds = (p * (dp - jnp.sum(p * dp, axis=0, keepdims=True))).astype(bf16)
            rows = slice(512 * r, 512 * r + 512)
            dkv_ref[rows, 256 * i : 256 * i + 256] = nn(
                ds, spread(q3_ref[64 * r : 64 * r + 64, cols], 64)
            ).astype(bf16)
            dkv_ref[rows, 512 + 256 * i : 512 + 256 * i + 256] = nn(
                p.astype(bf16), spread(do_r, 64)
            ).astype(bf16)
            dq.append(fold(tn(ds, k3), 64).astype(bf16))
        dq = jnp.concatenate(dq, axis=0)
        accs[i][at["cq"] : at["cq"] + 256] = one_grad(n3, dq)
        terms.append(two_back(dq, w.cq))
    part, dg2 = rms_back(z1, g2_ref[...], total(terms))
    dz1 = dz2 + part
    g = dz1.astype(bf16)
    z = x_ref[...].astype(f32)
    n2 = rms(z, g1_ref[...])
    mask = dec_self_mask(ids_ref, dseg_ref, rows_n)
    terms = []
    dtab = jnp.zeros((32, LANE), f32)
    out_lane = lax.broadcasted_iota(jnp.int32, (32, LANE), 1)
    onehot = dec_bucket_rows(buckets_ref)
    for i, (w, tab) in enumerate(zip(halves, (taba_ref[...], tabb_ref[:, 256:260]))):
        q, k, v = (qkv_ref[:, 512 * c + 256 * i : 512 * c + 256 * i + 256] for c in range(3))
        accs[i][at["out"] : at["out"] + 256] = tn(o2_ref[:, 256 * i : 256 * i + 256], g)
        do = nt(g, w.out()).astype(bf16)
        s = nn(k, spread_t(jnp.transpose(q), LANE)) + dec_bias_rows(tab, buckets_ref) + mask
        p = jnp.exp(s - lse_ref[i : i + 1, :])
        dp = nn(v, spread_t(jnp.transpose(do), LANE))
        ds = p * (dp - jnp.sum(p * dp, axis=0, keepdims=True))
        for h in range(4):
            diag = diagonal_sums(ds[:, LANE * h : LANE * h + LANE])
            col = jnp.sum(jnp.where(onehot, diag, 0.0), axis=1, keepdims=True)
            dtab = dtab + jnp.where(out_lane == 4 * i + h, col, 0.0)
        ds = ds.astype(bf16)
        dk = nn(ds, spread(q, LANE)).astype(bf16)
        dv = nn(p.astype(bf16), spread(do, LANE)).astype(bf16)
        dq = fold(tn(ds, k), LANE).astype(bf16)
        accs[i][at["qk"] : at["qk"] + 512, 0:256] = tn(n2, dq)
        accs[i][at["qk"] : at["qk"] + 512, 256:512] = tn(n2, dk)
        accs[i][at["v"] : at["v"] + 256] = one_grad(n2, dv)
        terms += [nt(dq, w.qk(0)), nt(dk, w.qk(1)), two_back(dv, w.v)]
    part, dg1 = rms_back(z, g1_ref[...], total(terms))
    dx_ref[...] = dz1 + part
    dg_ref[...] = jnp.concatenate([dg1, dg2, dg3], axis=0)
    dtab_ref[...] = dtab
    place(ids_ref, acc_a, ka_ref, sa_ref)
    place(ids_ref, acc_b, kb_ref, sb_ref)


def dec_main(x, cot, g1, g2, g3, buckets, dseg, seg, pad, ids, qkv, o2, lse, z1, q3, kv, taba, tabb, own, oth):
    n = x.shape[0]
    ins = [x, cot, g1, g2, g3, buckets, dseg, seg, pad, ids, qkv, o2, lse, z1, q3, kv, taba, tabb, *own, oth]
    half = dec_all.rows // 2
    outs = [
        sds((n, 512), bf16),
        sds((n, 512), f32),
        sds((kv.shape[0], 1024), bf16),
        sds((half, 512), bf16),
        sds((half, 512), bf16),
        sds((half, 512), bf16),
        sds((half, 512), bf16),
        sds((3, 512), f32),
        sds((32, LANE), f32),
    ]
    specs = [whole(a) for a in ins]
    specs[9] = smem
    return pl.pallas_call(
        dec_main_kernel,
        name="dec_cross_ff_back",
        grid=(1,),
        in_specs=specs,
        out_specs=[whole(a) for a in outs],
        out_shape=outs,
        scratch_shapes=[
            pltpu.VMEM((512, LANE), f32),
            pltpu.VMEM((4, 512, 256), f32),
            pltpu.VMEM((dec_all.rows, 512), f32),
            pltpu.VMEM((dec_all.rows, 512), f32),
        ],
        compiler_params=params(60),
        cost_estimate=cost(6e9, 2e7),
    )(*ins)


def natural(flat):
    shapes = {"out": (256, 512), "down": (1024, 512), "up": (512, 1024), "pair": (2, 512, 256), "one": (512, 256)}
    res = []
    for name, kind in flat.layout:
        if name == "qk":
            res.append(("q", (512, 256)))
        elif name == "v":
            res.append(("kv", (2, 512, 256)))
        else:
            res.append((name, shapes[kind]))
    return res


def finish_kernel(flat, ids_ref, a_ref, b_ref, *rest):
    outs, full = dict(zip([n for n, _ in natural(flat)], rest[:-1])), rest[-1]
    size = flat.rows // 16
    own = ids_ref[0]
    high = own // 8
    low = own % 8
    for j in range(16):
        at = pl.multiple_of(((j % 8) ^ low) * size, 16)

        @pl.when(high == j // 8)
        def _():
            full[j * size : (j + 1) * size] = a_ref[pl.ds(at, size), :].astype(f32)

        @pl.when(high != j // 8)
        def _():
            full[j * size : (j + 1) * size] = b_ref[pl.ds(at, size), :].astype(f32)

    for name, kind in flat.layout:
        row = flat.at[name][0]
        if name == "qk":
            outs["q"][...] = full[row : row + 512, :256]
            outs["kv"][0] = full[row : row + 512, 256:]
        elif name == "v":
            outs["kv"][1, :256] = full[row : row + 256, :256]
            outs["kv"][1, 256:] = full[row : row + 256, 256:]
        elif kind in ("out", "down"):
            outs[name][...] = full[row : row + outs[name].shape[0]]
        elif kind == "up":
            outs[name][:, :512] = full[row : row + 512]
            outs[name][:, 512:] = full[row + 512 : row + 1024]
        elif kind == "pair":
            outs[name][0] = full[row : row + 512, :256]
            outs[name][1] = full[row : row + 512, 256:]
        else:
            outs[name][:256] = full[row : row + 256, :256]
            outs[name][256:] = full[row : row + 256, 256:]


def finish(flat, ids, a, b):
    names = natural(flat)
    outs = [sds(shape, f32) for _, shape in names]
    res = pl.pallas_call(
        functools.partial(finish_kernel, flat),
        name="grads_out",
        grid=(1,),
        in_specs=[smem, whole(a), whole(b)],
        out_specs=[whole(o) for o in outs],
        out_shape=outs,
        scratch_shapes=[pltpu.VMEM((flat.rows, 512), f32)],
        compiler_params=params(),
        cost_estimate=cost(1e6, 6 * flat.rows * 512),
    )(ids, a, b)
    return {name: r for (name, _), r in zip(names, res)}


place_bits = 4


def swap_dp(a, bit):
    n = lax.axis_size("dp")
    return lax.ppermute(a, "dp", [(i, i ^ bit) for i in range(n)])


def swap_mp(a):
    return lax.ppermute(a, "mp", [(0, 1), (1, 0)])


def after(a, *others):
    return lax.optimization_barrier((a,) + others)[0]


def add_low(*terms):
    return total([t.astype(f32) for t in terms]).astype(bf16)


def reduce_other(pair_b):
    keep, send = pair_b
    return swap_mp(add_low(keep, swap_dp(send, 1)))


def reduce_own(pair_a, came):
    keep, send = pair_a
    cur = add_low(keep, swap_dp(send, 1), came)
    bits = [2, 4, 8]
    for bit in bits:
        n = cur.shape[0] // 2
        cur = add_low(cur[:n], swap_dp(cur[n:], bit))
    bit = 16
    while bit < lax.axis_size("dp"):
        cur = add_low(cur, swap_dp(cur, bit))
        bit *= 2
    for bit in bits[::-1]:
        cur = jnp.concatenate([cur, swap_dp(cur, bit)], axis=0)
    return cur, swap_dp(cur, 1)


def reduce_small(same, own, other):
    n = same.shape[0]
    cur = jnp.concatenate([same, own], axis=0) + swap_mp(jnp.concatenate([same, other], axis=0))
    bit = 1
    while bit < lax.axis_size("dp"):
        cur = cur + swap_dp(cur, bit)
        bit *= 2
    return cur[:n], cur[n:]


def on_device(
    enc_in,
    enc_segments,
    enc_pad,
    enc_buckets,
    dec_in,
    dec_segments,
    dec_buckets,
    enc_cot,
    dec_cot,
    enc_norm1,
    enc_query,
    enc_kv,
    enc_out_proj,
    enc_bias,
    enc_norm2,
    enc_ff_in,
    enc_ff_out,
    enc_final,
    dec_norm1,
    dec_query,
    dec_kv,
    dec_out_proj,
    dec_bias,
    dec_norm2,
    cross_query,
    cross_kv,
    cross_out,
    dec_norm3,
    dec_ff_in,
    dec_ff_out,
):
    rows, length, width = enc_in.shape
    dp = lax.axis_index("dp")
    core, y_at = dp % 2, dp // 2 % 2
    place_at = core * 8 + y_at * 4 + dp // 4 % 2 * 2 + dp // 8 % 2
    ids = jnp.stack([place_at, lax.axis_index("mp") * rows, core, core * 2 + y_at]).astype(jnp.int32)

    flat_qkv = enc_qkv_tabs.pack(
        {"qk": [enc_query, enc_kv[0]], "v": enc_kv[1], "tabs": [enc_bias, dec_bias]}
    )
    flat_mid = enc_mid.pack({"ffo": enc_ff_out, "ffi": enc_ff_in, "ckv": cross_kv, "out": enc_out_proj})
    flat_dec = dec_all.pack(
        {
            "ffo": dec_ff_out,
            "ffi": dec_ff_in,
            "cout": cross_out,
            "cq": cross_query,
            "out": dec_out_proj,
            "qk": [dec_query, dec_kv[0]],
            "v": dec_kv[1],
        }
    )

    def chunk(flat, at, n):
        size = flat.shape[0] // n
        return lax.dynamic_slice_in_dim(flat, at * size, size, 0)

    q0 = swap_mp(chunk(flat_qkv, core, 2))
    q1 = swap_dp(q0, 1)
    m0 = swap_mp(after(chunk(flat_mid, core * 2 + y_at, 4), q0))
    m1 = swap_dp(m0, 2)
    m2, m3 = swap_dp(m0, 1), swap_dp(m1, 1)
    d0 = swap_mp(after(chunk(flat_dec, core * 2 + y_at, 4), m0))
    d1 = swap_dp(after(d0, m1), 2)
    d2, d3 = swap_dp(d0, 1), swap_dp(d1, 1)

    n1g, n2g, nfg = enc_norm1[None, :], enc_norm2[None, :], enc_final[None, :]
    d1g, d2g, d3g = dec_norm1[None, :], dec_norm2[None, :], dec_norm3[None, :]
    rev = jnp.pad(enc_buckets[::-1], (0, 1), constant_values=-1)[None, :]
    places = dec_buckets[None, :]
    x = enc_in.reshape(rows * length, width)
    xc = enc_cot.reshape(rows * length, width)
    z = dec_in.reshape(-1, width)
    zc = dec_cot.reshape(-1, width)

    def flat2(a):
        return a.reshape(rows * length, a.shape[-1])

    qkv_a, o_a, lse_a = enc_fwd(
        ids, enc_in, n1g, enc_segments, enc_pad, rev, [enc_bias, enc_query, enc_kv]
    )
    qkv_b, o_b, lse_b, w_qkv, tabs = enc_fwd(ids, enc_in, n1g, enc_segments, enc_pad, rev, [q0, q1])
    own_mid = [enc_ff_out, enc_ff_in, cross_kv, enc_out_proj]
    x1, y, enc_out, h, slope, kv3, w_mid = mid_fwd(
        ids, x, flat2(o_a), flat2(o_b), n2g, nfg, own_mid, [m0, m1, m2, m3]
    )
    own_dec = [dec_ff_out, dec_ff_in, cross_out, cross_query, dec_out_proj, dec_query, dec_kv]
    dqkv, o2, lse2, z1, q3, w_dec = dec_first(
        ids, z, d1g, d2g, dec_segments, places, dec_bias, tabs, own_dec, [d0, d1, d2, d3]
    )
    dec_out, dec_grad, dkv3, dka, dsa, dkb, dsb, dgd, ddtab = dec_main(
        z, zc, d1g, d2g, d3g, places, dec_segments, enc_segments, enc_pad, ids,
        dqkv, o2, lse2, z1, q3, kv3, dec_bias, tabs, own_dec, w_dec,
    )
    came_dec = reduce_other((dkb, dsb))
    dec_a, dec_b = reduce_own((dka, dsa), came_dec)
    dx1, do, mka, msa, mkb, msb, dg2, dgf = mid_bwd(
        dkv3, y, xc, x1, h, slope, flat2(o_a), flat2(o_b), n2g, nfg, ids, own_mid, w_mid
    )
    came_mid = reduce_other((mkb, msb))
    mid_a, mid_b = reduce_own((mka, msa), came_mid)
    do = do.reshape(rows, length, width)
    dqkv_b, tkb, tsb, dtab_b = enc_bwd(
        1, ids, enc_in, n1g, enc_segments, enc_pad, rev, tabs, qkv_b, o_b, do, lse_b
    )
    came_qkv = reduce_other((tkb, tsb))
    dqkv_a, tka, tsa, dtab_a = enc_bwd(
        0, ids, enc_in, n1g, enc_segments, enc_pad, rev, enc_bias, qkv_a, o_a, do, lse_a
    )
    qkv_c, qkv_d = reduce_own((tka, tsa), came_qkv)
    enc_grad, dg1 = enc_last(x, dx1, flat2(dqkv_a), flat2(dqkv_b), n1g, [enc_query, enc_kv], w_qkv)
    same = jnp.concatenate([dg1, dg2, dgf, dgd], axis=0)
    tab_a = jnp.concatenate([dtab_a[:, 0:4], ddtab[:, 0:4]], axis=1)
    tab_b = jnp.concatenate([dtab_b[:, 0:4], ddtab[:, 4:8]], axis=1)
    same, tab = reduce_small(
        jnp.concatenate([same, jnp.zeros((2, width), f32)], axis=0),
        jnp.pad(tab_a, ((0, 0), (0, width - 8))),
        jnp.pad(tab_b, ((0, 0), (0, width - 8))),
    )
    dec_g = finish(dec_all, ids, dec_a, dec_b)
    mid_g = finish(enc_mid, ids, mid_a, mid_b)
    qkv_g = finish(enc_qkv, ids, qkv_c, qkv_d)
    return (
        enc_out.reshape(enc_in.shape),
        dec_out.reshape(dec_in.shape),
        enc_grad.reshape(enc_in.shape),
        dec_grad.reshape(dec_in.shape),
        same[0],
        qkv_g["q"],
        qkv_g["kv"],
        mid_g["out"],
        tab[:, 0:4],
        same[1],
        mid_g["ffi"],
        mid_g["ffo"],
        same[2],
        same[3],
        dec_g["q"],
        dec_g["kv"],
        dec_g["out"],
        tab[:, 4:8],
        same[4],
        dec_g["cq"],
        mid_g["ckv"],
        dec_g["cout"],
        same[5],
        dec_g["ffi"],
        dec_g["ffo"],
    )


def solution(mesh):
    in_specs = (
        P(("dp", "mp"), None, None),
        P("dp", None),
        P("dp", None),
        P(),
        P(("dp", "mp"), None, None),
        P("dp", None),
        P(),
        P(("dp", "mp"), None, None),
        P(("dp", "mp"), None, None),
        P(),
        P(None, "mp"),
        P(None, None, "mp"),
        P("mp", None),
        P(None, "mp"),
        P(),
        P(None, "mp"),
        P("mp", None),
        P(),
        P(),
        P(None, "mp"),
        P(None, None, "mp"),
        P("mp", None),
        P(None, "mp"),
        P(),
        P(None, "mp"),
        P(None, None, "mp"),
        P("mp", None),
        P(),
        P(None, "mp"),
        P("mp", None),
    )
    out_specs = (
        P(("dp", "mp"), None, None),
        P(("dp", "mp"), None, None),
        P(("dp", "mp"), None, None),
        P(("dp", "mp"), None, None),
        P(),
        P(None, "mp"),
        P(None, None, "mp"),
        P("mp", None),
        P(None, "mp"),
        P(),
        P(None, "mp"),
        P("mp", None),
        P(),
        P(),
        P(None, "mp"),
        P(None, None, "mp"),
        P("mp", None),
        P(None, "mp"),
        P(),
        P(None, "mp"),
        P(None, None, "mp"),
        P("mp", None),
        P(),
        P(None, "mp"),
        P("mp", None),
    )
    return jax.shard_map(
        on_device, mesh=mesh, in_specs=in_specs, out_specs=out_specs, check_vma=False
    )
```

time: 1340 us -> 416 us (0.31); the launches traced: 1320 us -> 412 us
  local copies, waits for them, and re-layouts: 517 us -> 25.4 us
  waiting for transfers between devices: 401 us -> 188 us
  matrix products: 177 us -> 0 us
  Pallas kernels: 0 us -> 146 us
  blocking collectives: 114 us -> 0 us
  other arithmetic: 91.6 us -> 17.4 us
  starting transfers between devices: 0.88 us -> 34.3 us
  between operations: 15.7 us -> 1.63 us
    psum x1 -> x0, waiting for transfers between devices: 188 us -> none  [on_device(): lax.psum((enc_query_grad, enc_kv_grad, enc_out_proj_grad, enc_bias_grad,...]
    ppermute x0 -> x45, waiting for transfers between devices: none -> 188 us  [the longest x38 103 us: swap_dp(): return lax.ppermute(a, 'dp', [(i, i ^ bit) for i in range(n)])]
    dot_general x83 -> x0, matrix products: 177 us -> none  [the longest x10 24.1 us: masked_scores(): jnp.einsum('qhd,khd->hqk', queries, key_rows, preferred_element_type=jnp....]
    pallas_call x0 -> x12, Pallas kernels: none -> 146 us  [the longest x1 31.3 us: mid_bwd(): pl.pallas_call(functools.partial(mid_bwd_kernel, n // tile), name='enc_mi...]
    rev x6 -> x0, local copies, waits for them, and re-layouts: 138 us -> none  [the longest x5 138 us: diagonal_totals(): flipped = score_block[:, ::-1, :]]
    reduce_scatter x11 -> x0, waiting for transfers between devices: 118 us -> none  [the longest x6 71.2 us: scatter_back(): lax.psum_scatter(term_rows(jnp.int32(0), lax.axis_size('mp') * row_count)...]
    while x32 -> x0, local copies, waits for them, and re-layouts: 110 us -> none
    all_gather x5 -> x0, waiting for transfers between devices: 94.2 us -> none  [the longest x3 54.9 us: spread_rows(): return lax.all_gather(values, 'mp', axis=0, tiled=True)]
  transfers between devices with their start and end apart: 17 -> 45, of which waited for: 11 -> 21; matrix products, arithmetic and copies ran while one was open for 44% -> 8% of each run, Pallas kernels for 0% -> 20%
where the time goes in v1:
time: 416 us; the launch traced here: 412 us
  waiting for transfers between devices  188 us (45%)
  Pallas kernels  146 us (35%)
  starting transfers between devices  34.3 us (8%)
  local copies, waits for them, and re-layouts  25.4 us (6%)
  other arithmetic  17.4 us (4%)
    ppermute x38, waiting for transfers between devices, swap_dp(): return lax.ppermute(a, 'dp', [(i, i ^ bit) for i in range(n)])  103 us
    ppermute x7, waiting for transfers between devices, swap_mp(): return lax.ppermute(a, 'mp', [(0, 1), (1, 0)])  84.6 us
    pallas_call x1, Pallas kernels, mid_bwd(): pl.pallas_call(functools.partial(mid_bwd_kernel, n // tile), name='enc_mi...  31.3 us
    ppermute x38, starting transfers between devices, swap_dp(): return lax.ppermute(a, 'dp', [(i, i ^ bit) for i in range(n)])  27.7 us
    pallas_call x2, Pallas kernels, enc_bwd(): pl.pallas_call(functools.partial(enc_bwd_kernel, rows), name='enc_attend_...  26.2 us
    pallas_call x2, Pallas kernels, enc_fwd(): pl.pallas_call(functools.partial(enc_fwd_kernel, own), name='enc_attend_o...  22.5 us
    pallas_call x1, Pallas kernels, dec_main(): pl.pallas_call(dec_main_kernel, name='dec_cross_ff_back', grid=(1,), in_s...  20.5 us
    pallas_call x1, Pallas kernels, mid_fwd(): pl.pallas_call(mid_fwd_kernel, name='enc_middle', grid=(n // tile,), in_s...  17.7 us
  transfers between devices with their start and end apart: 45, of which 21 were waited for; matrix products, arithmetic and copies ran while one was open for 8% of the time, Pallas kernels for 20%

profile of v1, /device:TPU:0, one launch (start us, length us, event | category | flops | bytes accessed | tf_op | source)
XLA Modules:
  0.0 412.5 jit_solution(8119858579666665390)
XLA Ops:
  25.4 12.5 %collective-permute-done.2.rest_4_ = bf16[704,512]{1,0:T(8,128)(2,1)S(1)} collective-permute-done((bf16[704,512]{1,0:T(8,128)(2,1)S(1)}, bf16[704,512]{1,0:T(8,128)(2,1)S(1)}, u32[]{:S(2)}, u32[]{:S(2)}) %collective-permute-start.2) | collective-permute-done | bytes 720928 | tf_op jit(solution)/shard_map/ppermute | solution.py:1067
  41.6 12.9 %collective-permute-done.3.rest_5_ = bf16[704,512]{1,0:T(8,128)(2,1)S(1)} collective-permute-done((bf16[704,512]{1,0:T(8,128)(2,1)S(1)}, bf16[704,512]{1,0:T(8,128)(2,1)S(1)}, u32[]{:S(2)}, u32[]{:S(2)}) %collective-permute-start.3) | collective-permute-done | bytes 720928 | tf_op jit(solution)/shard_map/ppermute | solution.py:1063
  54.5 4.2 %collective-permute-done.6.rest_7_ = bf16[896,512]{1,0:T(8,128)(2,1)S(1)} collective-permute-done((bf16[896,512]{1,0:T(8,128)(2,1)S(1)}, bf16[896,512]{1,0:T(8,128)(2,1)S(1)}, u32[]{:S(2)}, u32[]{:S(2)}) %collective-permute-start.6) | collective-permute-done | bytes 917536 | tf_op jit(solution)/shard_map/ppermute | solution.py:1067
  60.2 11.0 %enc_attend_own.1 = (bf16[2,512,768]{2,1,0:T(8,128)(2,1)}, bf16[2,512,256]{2,1,0:T(8,128)(2,1)}, f32[2,4,512]{2,1,0:T(4,128)}) custom-call(s32[4]{0:T(128)} %pad_add_fusion.ids_ref, bf16[2,512,512]{2,1,0:T(8,128)(2,1)} %x_ref.7, f32[1,512]{1,0:T(1,128)} %bitcast.80, s32[4,512]{1,0:T(4,128)} %seg_ref.9, s32[4,512]{1,0:T(4,128)} %pad_ref.9, ...), custom_call_target="tpu_custom_call" | custom-call | flops 8000000000 | bytes 4000000 | tf_op jit(solution)/shard_map/enc_attend_own/pallas_call | solution.py:263
  72.6 11.4 %enc_attend_other.1 = (bf16[2,512,768]{2,1,0:T(8,128)(2,1)}, bf16[2,512,256]{2,1,0:T(8,128)(2,1)}, f32[2,4,512]{2,1,0:T(4,128)}, bf16[800,512]{1,0:T(8,128)(2,1)}, bf16[32,512]{1,0:T(8,128)(2,1)}) custom-call(s32[4]{0:T(128)} %pad_add_fusion.ids_ref, bf16[2,512,512]{2,1,0:T(8,128)(2,1)} %x_ref.7, f32[1,512]{1,0:T(1,128)} %bitcast.81, s32[4,512]{1,0:T(4,128)} %seg_ref.9, ...), custom_call_target="tpu_custom_call" | custom-call | flops 8000000000 | bytes 4000000 | tf_op jit(solution)/shard_map/enc_attend_other/pallas_call | solution.py:263
  85.7 17.7 %enc_middle.1 = (f32[1024,512]{1,0:T(8,128)}, f32[1024,512]{1,0:T(8,128)}, bf16[1024,512]{1,0:T(8,128)(2,1)}, bf16[1024,2048]{1,0:T(8,128)(2,1)}, bf16[1024,2048...) custom-call(s32[4]{0:T(128)} %pad_add_fusion.ids_ref, bf16[1024,512]{1,0:T(8,128)(2,1)} %bitcast.72, ...), custom_call_target="tpu_custom_call" | custom-call | flops 10000000000 | bytes 20000000 | tf_op jit(solution)/shard_map/enc_middle/pallas_call | solution.py:512
  104.7 7.6 %dec_self.1 = (bf16[128,1536]{1,0:T(8,128)(2,1)}, bf16[128,512]{1,0:T(8,128)(2,1)}, f32[2,512]{1,0:T(2,128)}, f32[128,512]{1,0:T(8,128)}, bf16[128,512]{1,0:T(8,128)(2,1)}, /*index=5*/bf16[3584,512]{1,0:T(8,128)(2,1)}) custom-call(s32[4]{0:T(128)} %pad_add_fusion.ids_ref, bf16[128,512]{1,0:T(8,128)(2,1)} %bitcast.50, f32[1,512]{1,0:T(1,128)} %bitcast.59, ...), custom_call_target="tpu_custom_call" | custom-call | flops 1000000000 | bytes 8000000 | tf_op jit(solution)/shard_map/dec_self/pallas_call | solution.py:800
  112.3 20.5 %dec_cross_ff_back.1 = (bf16[128,512]{1,0:T(8,128)(2,1)}, f32[128,512]{1,0:T(8,128)}, bf16[1024,1024]{1,0:T(8,128)(2,1)}, bf16[1792,512]{1,0:T(8,128)(2,1)}, bf1...) custom-call(bf16[128,512]{1,0:T(8,128)(2,1)} %bitcast.51, ...), custom_call_target="tpu_custom_call" | custom-call | flops 6000000000 | bytes 20000000 | tf_op jit(solution)/shard_map/dec_cross_ff_back/pallas_call | solution.py:972
  132.9 31.3 %enc_middle_back.1 = (f32[1024,512]{1,0:T(8,128)}, bf16[1024,512]{1,0:T(8,128)(2,1)}, bf16[1408,512]{1,0:T(8,128)(2,1)}, bf16[1408,512]{1,0:T(8,128)(2,1)}, bf16...) custom-call(bf16[1024,1024]{1,0:T(8,128)(2,1)} %get-tuple-element.104.dkv_ref, ...), custom_call_target="tpu_custom_call" | custom-call | flops 22000001024 | bytes 30000000 | tf_op jit(solution)/shard_map/enc_middle_back/pallas_call | solution.py:611
  173.6 30.5 %collective-permute-done.27 = bf16[1408,512]{1,0:T(8,128)(2,1)S(1)} collective-permute-done((bf16[1408,512]{1,0:T(8,128)(2,1)S(1)}, bf16[1408,512]{1,0:T(8,128)(2,1)S(1)}, u32[]{:S(2)}, u32[]{:S(2)}) %collective-permute-start.27) | collective-permute-done | bytes 1441824 | tf_op jit(solution)/shard_map/ppermute | solution.py:1067
  205.3 37.4 %collective-permute-done.37 = bf16[1792,512]{1,0:T(8,128)(2,1)S(1)} collective-permute-done((bf16[1792,512]{1,0:T(8,128)(2,1)S(1)}, bf16[1792,512]{1,0:T(8,128)(2,1)S(1)}, u32[]{:S(2)}, u32[]{:S(2)}) %collective-permute-start.37) | collective-permute-done | bytes 1835040 | tf_op jit(solution)/shard_map/ppermute | solution.py:1067
  244.1 13.1 %enc_attend_other_back.1 = (bf16[2,512,768]{2,1,0:T(8,128)(2,1)}, bf16[384,512]{1,0:T(8,128)(2,1)}, bf16[384,512]{1,0:T(8,128)(2,1)}, f32[32,128]{1,0:T(8,128)}) custom-call(s32[4]{0:T(128)} %pad_add_fusion.ids_ref, bf16[2,512,512]{2,1,0:T(8,128)(2,1)} %x_ref.7, f32[1,512]{1,0:T(1,128)} %bitcast.82, s32[4,512]{1,0:T(4,128)} %seg_ref.9, s32[4,512]{1,0:T(4,128)} %pad_ref.9, ...), custom_call_target="tpu_custom_call" | custom-call | flops 16000000000 | bytes 8000000 | tf_op jit(solution)/shard_map/enc_attend_other_back/pallas_call | solution.py:410
  259.1 6.2 %collective-permute-done.38 = bf16[896,512]{1,0:T(8,128)(2,1)S(1)} collective-permute-done((bf16[896,512]{1,0:T(8,128)(2,1)S(1)}, bf16[896,512]{1,0:T(8,128)(2,1)S(1)}, u32[]{:S(2)}, u32[]{:S(2)}) %collective-permute-start.38) | collective-permute-done | bytes 917536 | tf_op jit(solution)/shard_map/ppermute | solution.py:1063
  267.2 13.1 %enc_attend_own_back.1 = (bf16[2,512,768]{2,1,0:T(8,128)(2,1)}, bf16[384,512]{1,0:T(8,128)(2,1)}, bf16[384,512]{1,0:T(8,128)(2,1)}, f32[32,128]{1,0:T(8,128)}) custom-call(s32[4]{0:T(128)} %pad_add_fusion.ids_ref, bf16[2,512,512]{2,1,0:T(8,128)(2,1)} %x_ref.7, f32[1,512]{1,0:T(1,128)} %bitcast.83, s32[4,512]{1,0:T(4,128)} %seg_ref.9, s32[4,512]{1,0:T(4,128)} %pad_ref.9, ...), custom_call_target="tpu_custom_call" | custom-call | flops 16000000000 | bytes 8000000 | tf_op jit(solution)/shard_map/enc_attend_own_back/pallas_call | solution.py:410
  283.8 14.5 %collective-permute-done.40 = bf16[224,512]{1,0:T(8,128)(2,1)S(1)} collective-permute-done((bf16[224,512]{1,0:T(8,128)(2,1)S(1)}, bf16[224,512]{1,0:T(8,128)(2,1)S(1)}, u32[]{:S(2)}, u32[]{:S(2)}) %collective-permute-start.40) | collective-permute-done | bytes 229408 | tf_op jit(solution)/shard_map/ppermute | solution.py:1063
  298.9 13.0 %collective-permute-done.41 = bf16[224,512]{1,0:T(8,128)(2,1)S(1)} collective-permute-done((bf16[224,512]{1,0:T(8,128)(2,1)S(1)}, bf16[224,512]{1,0:T(8,128)(2,1)S(1)}, u32[]{:S(2)}, u32[]{:S(2)}) %collective-permute-start.41) | collective-permute-done | bytes 229408 | tf_op jit(solution)/shard_map/ppermute | solution.py:1063
  312.1 3.2 collective-permute-start.31
  315.3 6.8 %enc_input_back.1 = (f32[1024,512]{1,0:T(8,128)}, f32[1,512]{1,0:T(1,128)}) custom-call(bf16[1024,512]{1,0:T(8,128)(2,1)} %bitcast.73, f32[1024,512]{1,0:T(8,128)} %get-tuple-element.110.dx1_ref, bf16[1024,768]{1,0:T(8,128)(2,1)} %bitcast.87, bf16[1024,768]{1,0:T(8,128)(2,1)} %bitcast.86, f32[1,512]{1,0:T(1,128)} %bitcast.84, bf16[512,256]{1,0:T(8,128)(2,1)} %wq_ref.1, ...), custom_call_target="tpu_custom_call" | custom-call | flops 4000000000 | bytes 10000000 | tf_op jit(solution)/shard_map/enc_input_back/pallas_call | solution.py:666
  322.1 6.3 %collective-permute-done.42 = bf16[448,512]{1,0:T(8,128)(2,1)S(1)} collective-permute-done((bf16[448,512]{1,0:T(8,128)(2,1)S(1)}, bf16[448,512]{1,0:T(8,128)(2,1)S(1)}, u32[]{:S(2)}, u32[]{:S(2)}) %collective-permute-start.42) | collective-permute-done | bytes 458784 | tf_op jit(solution)/shard_map/ppermute | solution.py:1063
  331.8 7.4 %collective-permute-done.32 = bf16[352,512]{1,0:T(8,128)(2,1)S(1)} collective-permute-done((bf16[352,512]{1,0:T(8,128)(2,1)}, bf16[352,512]{1,0:T(8,128)(2,1)S(1)}, u32[]{:S(2)}, u32[]{:S(2)}) %collective-permute-start.32) | collective-permute-done | bytes 360480 | tf_op jit(solution)/shard_map/ppermute | solution.py:1063
  340.9 15.2 %collective-permute-done.18 = bf16[192,512]{1,0:T(8,128)(2,1)} collective-permute-done((bf16[192,512]{1,0:T(8,128)(2,1)S(1)}, bf16[192,512]{1,0:T(8,128)(2,1)}, u32[]{:S(2)}, u32[]{:S(2)}) %collective-permute-start.18) | collective-permute-done | bytes 196640 | tf_op jit(solution)/shard_map/ppermute | solution.py:1063
  362.7 7.0 %collective-permute-done.33 = bf16[704,512]{1,0:T(8,128)(2,1)S(1)} collective-permute-done((bf16[704,512]{1,0:T(8,128)(2,1)S(1)}, bf16[704,512]{1,0:T(8,128)(2,1)S(1)}, u32[]{:S(2)}, u32[]{:S(2)}) %collective-permute-start.33) | collective-permute-done | bytes 720928 | tf_op jit(solution)/shard_map/ppermute | solution.py:1063
  401.5 4.9 %grads_out.4 = (f32[1024,512]{1,0:T(8,128)}, f32[512,1024]{1,0:T(8,128)}, f32[2,512,256]{2,1,0:T(8,128)}, f32[256,512]{1,0:T(8,128)}) custom-call(s32[4]{0:T(128)} %pad_add_fusion.ids_ref, bf16[1408,512]{1,0:T(8,128)(2,1)} %copy-done.1, bf16[1408,512]{1,0:T(8,128)(2,1)} %collective-permute-done.34.b_ref), custom_call_target="tpu_custom_call" | custom-call | flops 1000000 | bytes 8650752 | tf_op jit(solution)/shard_map/grads_out/pallas_call | solution.py:1044
  406.5 5.8 %grads_out.5 = (f32[1024,512]{1,0:T(8,128)}, f32[512,1024]{1,0:T(8,128)}, f32[256,512]{1,0:T(8,128)}, f32[512,256]{1,0:T(8,128)}, f32[256,512]{1,0:T(8,128)}, /*...) custom-call(s32[4]{0:T(128)} %pad_add_fusion.ids_ref, bf16[1792,512]{1,0:T(8,128)(2,1)} %copy-done, ...), custom_call_target="tpu_custom_call" | custom-call | flops 1000000 | bytes 11010048 | tf_op jit(solution)/shard_map/grads_out/pallas_call | solution.py:1044
  (248 shorter events, 97.2 us)
Async XLA Ops:
  20.3 17.6 %collective-permute-start.2 = (bf16[704,512]{1,0:T(8,128)(2,1)S(1)}, bf16[704,512]{1,0:T(8,128)(2,1)S(1)}, u32[]{:S(2)}, u32[]{:S(2)}) collective-permute-start(bf16[704,512]{1,0:T(8,128)(2,1)S(1)} %constant_dynamic-slice_fusion.1), channel_id=1, source_target_pairs={{0,1},{1,0},{2,3},{3,2},{4,5},{5,4},{6,7},{7,6},{8,9},{9,8},{10,11... | collective-permute-start | bytes 2162696 | tf_op jit(solution)/shard_map/ppermute | solution.py:1067
  37.9 20.8 %collective-permute-start.6 = (bf16[896,512]{1,0:T(8,128)(2,1)S(1)}, bf16[896,512]{1,0:T(8,128)(2,1)S(1)}, u32[]{:S(2)}, u32[]{:S(2)}) collective-permute-start(bf16[896,512]{1,0:T(8,128)(2,1)S(1)} %constant_dynamic-slice_fusion), channel_id=1, source_target_pairs={{0,1},{1,0},{2,3},{3,2},{4,5},{5,4},{6,7},{7,6},{8,9},{9,8},{10,11... | collective-permute-start | bytes 2752520 | tf_op jit(solution)/shard_map/ppermute | solution.py:1067
  41.6 30.2 %collective-permute-start.1 = (bf16[400,512]{1,0:T(8,128)(2,1)}, bf16[400,512]{1,0:T(8,128)(2,1)S(1)}, u32[]{:S(2)}, u32[]{:S(2)}) collective-permute-start(bf16[400,512]{1,0:T(8,128)(2,1)} %collective-permute-done.rest_0_), channel_id=1, source_target_pairs={{0,2},{2,0},{4,6},{6,4},{8,10},{10,8},{12,14},{14,12},{16,18},{18,... | collective-permute-start | bytes 1228808 | tf_op jit(solution)/shard_map/ppermute | solution.py:1063
  58.7 25.5 %collective-permute-start.7 = (bf16[896,512]{1,0:T(8,128)(2,1)S(1)}, bf16[896,512]{1,0:T(8,128)(2,1)S(1)}, u32[]{:S(2)}, u32[]{:S(2)}) collective-permute-start(bf16[896,512]{1,0:T(8,128)(2,1)S(1)} %collective-permute-done.6.rest_7_), channel_id=1, source_target_pairs={{0,4},{2,6},{4,0},{6,2},{8,12},{10,14},{12,8},{14,10},{16,20},{18,... | collective-permute-start | bytes 2752520 | tf_op jit(solution)/shard_map/ppermute | solution.py:1063
  84.0 19.4 %collective-permute-start.8 = (bf16[896,512]{1,0:T(8,128)(2,1)S(1)}, bf16[896,512]{1,0:T(8,128)(2,1)S(1)}, u32[]{:S(2)}, u32[]{:S(2)}) collective-permute-start(bf16[896,512]{1,0:T(8,128)(2,1)S(1)} %collective-permute-done.6.rest_7_), channel_id=1, source_target_pairs={{0,2},{2,0},{4,6},{6,4},{8,10},{10,8},{12,14},{14,12},{16,18},{18,... | collective-permute-start | bytes 2752520 | tf_op jit(solution)/shard_map/ppermute | solution.py:1063
  84.2 19.3 %collective-permute-start.9 = (bf16[896,512]{1,0:T(8,128)(2,1)S(1)}, bf16[896,512]{1,0:T(8,128)(2,1)S(1)}, u32[]{:S(2)}, u32[]{:S(2)}) collective-permute-start(bf16[896,512]{1,0:T(8,128)(2,1)S(1)} %collective-permute-done.7.rest_8_), channel_id=1, source_target_pairs={{0,2},{2,0},{4,6},{6,4},{8,10},{10,8},{12,14},{14,12},{16,18},{18,... | collective-permute-start | bytes 2752520 | tf_op jit(solution)/shard_map/ppermute | solution.py:1063
  165.0 40.3 %collective-permute-start.35 = (bf16[1792,512]{1,0:T(8,128)(2,1)}, bf16[1792,512]{1,0:T(8,128)(2,1)S(1)}, u32[]{:S(2)}, u32[]{:S(2)}) collective-permute-start(bf16[1792,512]{1,0:T(8,128)(2,1)} %get-tuple-element.142), channel_id=1, source_target_pairs={{0,2},{2,0},{4,6},{6,4},{8,10},{10,8},{12,14},{14,12},{16,18},{18,... | collective-permute-start | bytes 5505032 | tf_op jit(solution)/shard_map/ppermute | solution.py:1063
  169.6 34.5 %collective-permute-start.27 = (bf16[1408,512]{1,0:T(8,128)(2,1)S(1)}, bf16[1408,512]{1,0:T(8,128)(2,1)S(1)}, u32[]{:S(2)}, u32[]{:S(2)}) collective-permute-start(bf16[1408,512]{1,0:T(8,128)(2,1)S(1)} %add_convert_fusion.3), channel_id=1, source_target_pairs={{0,1},{1,0},{2,3},{3,2},{4,5},{5,4},{6,7},{7,6},{8,9},{9,8},{10,11... | collective-permute-start | bytes 4325384 | tf_op jit(solution)/shard_map/ppermute | solution.py:1067
  173.3 69.5 %collective-permute-start.37 = (bf16[1792,512]{1,0:T(8,128)(2,1)S(1)}, bf16[1792,512]{1,0:T(8,128)(2,1)S(1)}, u32[]{:S(2)}, u32[]{:S(2)}) collective-permute-start(bf16[1792,512]{1,0:T(8,128)(2,1)S(1)} %add_convert_fusion.1), channel_id=1, source_target_pairs={{0,1},{1,0},{2,3},{3,2},{4,5},{5,4},{6,7},{7,6},{8,9},{9,8},{10,11... | collective-permute-start | bytes 5505032 | tf_op jit(solution)/shard_map/ppermute | solution.py:1067
  204.8 52.5 %collective-permute-start.28 = (bf16[704,512]{1,0:T(8,128)(2,1)S(1)}, bf16[704,512]{1,0:T(8,128)(2,1)S(1)}, u32[]{:S(2)}, u32[]{:S(2)}) collective-permute-start(bf16[704,512]{1,0:T(8,128)(2,1)S(1)} %slice.216), channel_id=1, source_target_pairs={{0,4},{2,6},{4,0},{6,2},{8,12},{10,14},{12,8},{14,10},{16,20},{18,... | collective-permute-start | bytes 2162696 | tf_op jit(solution)/shard_map/ppermute | solution.py:1063
  243.6 21.7 %collective-permute-start.38 = (bf16[896,512]{1,0:T(8,128)(2,1)S(1)}, bf16[896,512]{1,0:T(8,128)(2,1)S(1)}, u32[]{:S(2)}, u32[]{:S(2)}) collective-permute-start(bf16[896,512]{1,0:T(8,128)(2,1)S(1)} %slice.226), channel_id=1, source_target_pairs={{0,4},{2,6},{4,0},{6,2},{8,12},{10,14},{12,8},{14,10},{16,20},{18,... | collective-permute-start | bytes 2752520 | tf_op jit(solution)/shard_map/ppermute | solution.py:1063
  257.2 41.2 %collective-permute-start.16 = (bf16[384,512]{1,0:T(8,128)(2,1)}, bf16[384,512]{1,0:T(8,128)(2,1)S(1)}, u32[]{:S(2)}, u32[]{:S(2)}) collective-permute-start(bf16[384,512]{1,0:T(8,128)(2,1)} %get-tuple-element.131), channel_id=1, source_target_pairs={{0,2},{2,0},{4,6},{6,4},{8,10},{10,8},{12,14},{14,12},{16,18},{18,... | collective-permute-start | bytes 1179656 | tf_op jit(solution)/shard_map/ppermute | solution.py:1063
  257.5 25.8 %collective-permute-start.29 = (bf16[352,512]{1,0:T(8,128)(2,1)S(1)}, bf16[352,512]{1,0:T(8,128)(2,1)S(1)}, u32[]{:S(2)}, u32[]{:S(2)}) collective-permute-start(bf16[352,512]{1,0:T(8,128)(2,1)S(1)} %slice.218), channel_id=1, source_target_pairs={{0,8},{2,10},{4,12},{6,14},{8,0},{10,2},{12,4},{14,6},{16,24},{18,... | collective-permute-start | bytes 1081352 | tf_op jit(solution)/shard_map/ppermute | solution.py:1063
  280.4 49.9 %collective-permute-start.15 = (bf16[384,512]{1,0:T(8,128)(2,1)}, bf16[384,512]{1,0:T(8,128)(2,1)S(1)}, u32[]{:S(2)}, u32[]{:S(2)}) collective-permute-start(bf16[384,512]{1,0:T(8,128)(2,1)} %get-tuple-element.129), channel_id=1, source_target_pairs={{0,2},{2,0},{4,6},{6,4},{8,10},{10,8},{12,14},{14,12},{16,18},{18,... | collective-permute-start | bytes 1179656 | tf_op jit(solution)/shard_map/ppermute | solution.py:1063
  280.6 17.7 %collective-permute-start.40 = (bf16[224,512]{1,0:T(8,128)(2,1)S(1)}, bf16[224,512]{1,0:T(8,128)(2,1)S(1)}, u32[]{:S(2)}, u32[]{:S(2)}) collective-permute-start(bf16[224,512]{1,0:T(8,128)(2,1)S(1)} %slice.230), channel_id=1, source_target_pairs={{0,16},{2,18},{4,20},{6,22},{8,24},{10,26},{12,28},{14,30},{16,0},... | collective-permute-start | bytes 688136 | tf_op jit(solution)/shard_map/ppermute | solution.py:1063
  283.4 28.7 %collective-permute-start.30 = (bf16[176,512]{1,0:T(8,128)(2,1)S(1)}, bf16[176,512]{1,0:T(8,128)(2,1)S(1)}, u32[]{:S(2)}, u32[]{:S(2)}) collective-permute-start(bf16[176,512]{1,0:T(8,128)(2,1)S(1)} %slice.220), channel_id=1, source_target_pairs={{0,16},{2,18},{4,20},{6,22},{8,24},{10,26},{12,28},{14,30},{16,0},... | collective-permute-start | bytes 540680 | tf_op jit(solution)/shard_map/ppermute | solution.py:1063
  298.5 31.7 %collective-permute-start.17 = (bf16[384,512]{1,0:T(8,128)(2,1)S(1)}, bf16[384,512]{1,0:T(8,128)(2,1)S(1)}, u32[]{:S(2)}, u32[]{:S(2)}) collective-permute-start(bf16[384,512]{1,0:T(8,128)(2,1)S(1)} %add_convert_fusion.8), channel_id=1, source_target_pairs={{0,1},{1,0},{2,3},{3,2},{4,5},{5,4},{6,7},{7,6},{8,9},{9,8},{10,11... | collective-permute-start | bytes 1179656 | tf_op jit(solution)/shard_map/ppermute | solution.py:1067
  312.0 16.4 %collective-permute-start.42 = (bf16[448,512]{1,0:T(8,128)(2,1)S(1)}, bf16[448,512]{1,0:T(8,128)(2,1)S(1)}, u32[]{:S(2)}, u32[]{:S(2)}) collective-permute-start(bf16[448,512]{1,0:T(8,128)(2,1)S(1)} %pad_maximum_fusion.4), channel_id=1, source_target_pairs={{0,8},{2,10},{4,12},{6,14},{8,0},{10,2},{12,4},{14,6},{16,24},{18,... | collective-permute-start | bytes 1376264 | tf_op jit(solution)/shard_map/ppermute | solution.py:1063
  312.1 16.9 %collective-permute-start.31 = (bf16[176,512]{1,0:T(8,128)(2,1)S(1)}, bf16[176,512]{1,0:T(8,128)(2,1)S(1)}, u32[]{:S(2)}, u32[]{:S(2)}) collective-permute-start(bf16[176,512]{1,0:T(8,128)(2,1)S(1)} %add_convert_fusion.12), channel_id=1, source_target_pairs={{0,16},{2,18},{4,20},{6,22},{8,24},{10,26},{12,28},{14,30},{16,0},... | collective-permute-start | bytes 540680 | tf_op jit(solution)/shard_map/ppermute | solution.py:1063
  328.4 28.8 %collective-permute-start.43 = (bf16[896,512]{1,0:T(8,128)(2,1)S(1)}, bf16[896,512]{1,0:T(8,128)(2,1)}, u32[]{:S(2)}, u32[]{:S(2)}) collective-permute-start(bf16[896,512]{1,0:T(8,128)(2,1)S(1)} %pad_maximum_fusion.2), channel_id=1, source_target_pairs={{0,4},{2,6},{4,0},{6,2},{8,12},{10,14},{12,8},{14,10},{16,20},{18,... | collective-permute-start | bytes 2752520 | tf_op jit(solution)/shard_map/ppermute | solution.py:1063
  330.4 25.7 %collective-permute-start.18 = (bf16[192,512]{1,0:T(8,128)(2,1)S(1)}, bf16[192,512]{1,0:T(8,128)(2,1)}, u32[]{:S(2)}, u32[]{:S(2)}) collective-permute-start(bf16[192,512]{1,0:T(8,128)(2,1)S(1)} %slice.210), channel_id=1, source_target_pairs={{0,4},{2,6},{4,0},{6,2},{8,12},{10,14},{12,8},{14,10},{16,20},{18,... | collective-permute-start | bytes 589832 | tf_op jit(solution)/shard_map/ppermute | solution.py:1063
  339.3 30.3 %collective-permute-start.33 = (bf16[704,512]{1,0:T(8,128)(2,1)S(1)}, bf16[704,512]{1,0:T(8,128)(2,1)S(1)}, u32[]{:S(2)}, u32[]{:S(2)}) collective-permute-start(bf16[704,512]{1,0:T(8,128)(2,1)S(1)} %pad_maximum_fusion.3), channel_id=1, source_target_pairs={{0,4},{2,6},{4,0},{6,2},{8,12},{10,14},{12,8},{14,10},{16,20},{18,... | collective-permute-start | bytes 2162696 | tf_op jit(solution)/shard_map/ppermute | solution.py:1063
  358.7 47.8 %collective-permute-start.44 = (bf16[1792,512]{1,0:T(8,128)(2,1)S(1)}, bf16[1792,512]{1,0:T(8,128)(2,1)}, u32[]{:S(2)}, u32[]{:S(2)}) collective-permute-start(bf16[1792,512]{1,0:T(8,128)(2,1)S(1)} %pad_maximum_fusion.a_ref), channel_id=1, source_target_pairs={{0,2},{2,0},{4,6},{6,4},{8,10},{10,8},{12,14},{14,12},{16,18},{18,... | collective-permute-start | bytes 5505032 | tf_op jit(solution)/shard_map/ppermute | solution.py:1063
  369.8 31.7 %collective-permute-start.34 = (bf16[1408,512]{1,0:T(8,128)(2,1)S(1)}, bf16[1408,512]{1,0:T(8,128)(2,1)}, u32[]{:S(2)}, u32[]{:S(2)}) collective-permute-start(bf16[1408,512]{1,0:T(8,128)(2,1)S(1)} %pad_maximum_fusion.1.a_ref), channel_id=1, source_target_pairs={{0,2},{2,0},{4,6},{6,4},{8,10},{10,8},{12,14},{14,12},{16,18},{18,... | collective-permute-start | bytes 4325384 | tf_op jit(solution)/shard_map/ppermute | solution.py:1063
  (64 other events, 694.4 us)
